TPU v7x, 128 devices: a whole 4x4x4 slice. The times are simulated.
128 devices in a mesh: grp: 4 (over z), dev: 32 (over x, y, core).
Axes of the slice: x: 4, y: 4, z: 4, core: 2. Of those that a mesh axis runs over, the one named last changes fastest.
Arguments:
- a_blocks: bfloat16 [16384, 64, 512], P(('grp', 'dev')), may hold values from -0.25 to 0.25
- a_cols: int32 [16384, 8], P(('grp', 'dev')), may hold values from 0 to 16383, as said below
- p_blocks: bfloat16 [16384, 64, 256], P(('grp', 'dev')), may hold values from -0.75 to 0.75
- ap_slots: int32 [16384, 32], P(('grp', 'dev')), may hold values from 0 to 7
- p_touch: int32 [16384, 4], P(('grp', 'dev')), may hold values from 0 to 223
- owner_dev: int32 [28672, 1], P(('grp', 'dev')), may hold values from 0 to 127, as said below
- owner_row: int32 [28672], P(('grp', 'dev')), may hold values from 0 to 7
Outputs:
- coarse: bfloat16 [1024, 64, 512], P('dev')
Inputs may be any that keep to these rules, and one draw needn't show every extreme that they name: `a_cols`: entries 0 to 5 of a row name fine rows of the same device; entry 6 names one of the last 32 rows of the device before it, entry 7 one of the first 32 rows of the device after it (rows of the same device on the first and last device). `owner_dev`: the owner of a column of device q is q, q - 1 or q + 1; at most 28 of the 224 columns of one device are owned by q - 1, and at most 28 by q + 1, and some device reaches 28 on each side.
All inputs are finite; a program needn't handle non-finite values.
Results may differ from a plain program's by a relative error of at most 0.006.
Values may be sent and summed in bfloat16 or wider, within the bound.
A program may use at most 256 MiB of HBM per device.

v0:
```python
import jax
import jax.numpy as jnp
from jax import lax
from jax.sharding import PartitionSpec as P

BS = 64
KA = 8
KP = 4
KC = 8
CB = 8
NT = 224
CAP = 28


def with_halo(value, sides, width):
    for axis, dim in sides:
        size, length = (lax.axis_size(axis), value.shape[dim])
        up = [(i, (i + 1) % size) for i in range(size - 1)]
        down = [(j, i) for i, j in up]
        last = lax.slice_in_dim(value, length - width, length, axis=dim)
        first = lax.slice_in_dim(value, 0, width, axis=dim)
        before = lax.ppermute(last, axis, up)
        after = lax.ppermute(first, axis, down)
        value = jnp.concatenate([before, value, after], axis=dim)
    return value


def shifted(value, axis, by):
    length = lax.axis_size(axis)
    pairs = [(i, i + by) for i in range(length) if 0 <= i + by < length]
    return lax.ppermute(value, axis, pairs)


def on_device(a_blocks, a_cols, p_blocks, ap_slots, p_touch, owner_dev, owner_row):
    fine_rows = a_blocks.shape[0]
    position = lax.axis_index(("grp", "dev"))
    window = with_halo(p_blocks, ((("grp", "dev"), 0),), fine_rows)
    local_cols = a_cols - position * fine_rows + fine_rows
    block_rows = 16
    steps_count = fine_rows // block_rows

    def add_block(partial_value, block_in):
        a_part, col_part, slot_part, touch_part, p_part = block_in
        nearby = window[col_part]
        products = jnp.einsum(
            "iakb,ikbn->ikan",
            a_part.reshape(block_rows, BS, KA, BS),
            nearby,
            preferred_element_type=jnp.float32,
        )
        products = products.reshape(block_rows, KA, BS, KP, BS)
        onehot = (slot_part.reshape(block_rows, KA, KP)[..., None] == jnp.arange(KC)).astype(
            jnp.float32
        )
        assembled = jnp.einsum(
            "ikms,ikamc->iasc", onehot, products, precision=lax.Precision.HIGHEST
        )
        rounded = assembled.reshape(block_rows, BS, KC * BS).astype(jnp.bfloat16)
        pieces = jnp.einsum(
            "iamb,ian->imbn",
            p_part.reshape(block_rows, BS, KP, BS),
            rounded,
            preferred_element_type=jnp.float32,
        )
        added = jax.ops.segment_sum(
            pieces.reshape(block_rows * KP, BS, KC * BS), touch_part.reshape(-1), num_segments=NT
        )
        return (partial_value + added, None)

    inputs = (
        a_blocks.reshape(steps_count, block_rows, BS, KA * BS),
        local_cols.reshape(steps_count, block_rows, KA),
        ap_slots.reshape(steps_count, block_rows, KA * KP),
        p_touch.reshape(steps_count, block_rows, KP),
        p_blocks.reshape(steps_count, block_rows, BS, KP * BS),
    )
    start = jnp.zeros((NT, BS, KC * BS), jnp.float32)
    summed, _ = lax.scan(add_block, start, inputs)
    summed = summed.astype(jnp.bfloat16)
    targets = owner_dev[:, 0]
    row_range = jnp.arange(CB)

    def slots_for(dest):
        chosen = targets == dest
        order_in = jnp.cumsum(chosen.astype(jnp.int32)) - 1
        matches = chosen[None, :] & (order_in[None, :] == jnp.arange(CAP)[:, None])
        data = jnp.einsum(
            "ct,tan->can", matches.astype(jnp.bfloat16), summed, preferred_element_type=jnp.float32
        ).astype(jnp.bfloat16)
        picked = jnp.sum(matches.astype(jnp.int32) * owner_row[None, :], axis=1)
        slot_rows = jnp.where(jnp.any(matches, axis=1), picked, CB)
        return (data, slot_rows)

    def place(data, slot_rows):
        selector = (slot_rows[None, :] == row_range[:, None]).astype(jnp.bfloat16)
        return jnp.einsum("ru,uan->ran", selector, data, preferred_element_type=jnp.float32)

    chosen = (targets == position)[None, :] & (owner_row[None, :] == row_range[:, None])
    owned = jnp.einsum(
        "rt,tan->ran", chosen.astype(jnp.bfloat16), summed, preferred_element_type=jnp.float32
    )
    next_data, next_rows = slots_for(position + 1)
    prev_data, prev_rows = slots_for(position - 1)
    from_prev, from_prev_rows = shifted((next_data, next_rows), ("grp", "dev"), 1)
    from_next, from_next_rows = shifted((prev_data, prev_rows), ("grp", "dev"), -1)
    owned = owned + place(from_prev, from_prev_rows) + place(from_next, from_next_rows)
    owned = owned.astype(jnp.bfloat16)
    return lax.all_gather(owned, "grp", axis=0, tiled=True)


def solution(mesh):
    placed = (
        P(("grp", "dev"), None, None),
        P(("grp", "dev"), None),
        P(("grp", "dev"), None, None),
        P(("grp", "dev"), None),
        P(("grp", "dev"), None),
        P(("grp", "dev"), None),
        P(("grp", "dev")),
    )
    return jax.shard_map(
        on_device, mesh=mesh, in_specs=placed, out_specs=P("dev", None, None), check_vma=False
    )
```

profile of v0, /device:TPU:0, one launch (start us, length us, event | category | flops | bytes accessed | tf_op | source)
XLA Modules:
  0.0 815.3 jit_solution(657119378494754312)
XLA Ops:
  24.8 11.6 %pad_maximum_fusion = bf16[384,64,256]{2,1,0:T(8,128)(2,1)} fusion(bf16[128,64,256]{2,1,0:T(8,128)(2,1)} %collective-permute-done.1, bf16[128,64,256]{2,1,0:T(8,128)(2,1)} %param.11, bf16[128,64,256]{2,1,0:T(8,128)(2,1)} %collective-permute-done), kind=kLoop, calls=%fused_computation.18 | loop fusion | flops 12582912 | bytes 25165824 | tf_op jit(solution)/shard_map/concatenate | solution.py:24
  36.4 13.5 %broadcast.68 = f32[224,64,512]{2,1,0:T(8,128)} broadcast(f32[]{:T(128)} %constant.49.clone.1), dimensions={} | broadcast | bytes 29360132 | tf_op jit(solution)/shard_map/broadcast.9
  49.8 614.8 %while.10 = (s32[]{:T(128)}, f32[224,64,512]{2,1,0:T(8,128)}, s32[8,16,4]{2,1,0:T(8,128)S(1)}, bf16[8,16,64,256]{2,3,1,0:T(8,128)(2,1)}, bf16[8,16,64,512]{3,2,1...) while((s32[]{:T(128)}, f32[224,64,512]{2,1,0:T(8,128)}, ...), condition=%wide.region_2.3_spmd, body=%wide.region_0.2_spmd.sunk | while | flops 740824448 | bytes 90726776 | solution.py:78
  70.6 14.8 %reshape.181 = f32[16,8,64,4,64]{4,3,2,1,0:T(4,128)} reshape(f32[16,8,64,256]{3,2,1,0:T(8,128)} %fusion.76) | data formatting | bytes 16777216 | tf_op jit(solution)/shard_map/while/body/eval_jaxpr/reshape | solution.py:51
  85.6 13.6 %fusion.77 = bf16[16,64,8,64]{3,2,1,0:T(8,128)(2,1)S(1)} fusion(f32[16,8,64,4,64]{4,3,2,1,0:T(4,128)} %reshape.181, s32[16,8,4]{2,1,0:T(8,128)S(1)} %copy.88), kind=kOutput, calls=%fused_computation.5.clone.1 | convolution fusion | flops 201854976 | bytes 9439232 | tf_op jit(solution)/shard_map/while/body/eval_jaxpr/ikms,ikamc->iasc/dot_general | solution.py:55
  107.1 19.9 %scatter_fusion = f32[224,64,512]{2,1,0:T(8,128)} fusion(f32[224,64,512]{2,1,0:T(8,128)} %get-tuple-element.154, s32[64]{0:T(128)S(1)} %reshape.178, f32[64,64,512]{2,1,0:T(8,128)} %bitcast.90), kind=kCustom, calls=%fused_computation.1.clone.1 | custom fusion | flops 2097152 | bytes 25166080 | tf_op jit(solution)/shard_map/while/body/eval_jaxpr/scatter-add | solution.py:65
  147.5 14.8 %reshape.181 = f32[16,8,64,4,64]{4,3,2,1,0:T(4,128)} reshape(f32[16,8,64,256]{3,2,1,0:T(8,128)} %fusion.76) | data formatting | bytes 16777216 | tf_op jit(solution)/shard_map/while/body/eval_jaxpr/reshape | solution.py:51
  162.6 13.6 %fusion.77 = bf16[16,64,8,64]{3,2,1,0:T(8,128)(2,1)S(1)} fusion(f32[16,8,64,4,64]{4,3,2,1,0:T(4,128)} %reshape.181, s32[16,8,4]{2,1,0:T(8,128)S(1)} %copy.88), kind=kOutput, calls=%fused_computation.5.clone.1 | convolution fusion | flops 201854976 | bytes 9439232 | tf_op jit(solution)/shard_map/while/body/eval_jaxpr/ikms,ikamc->iasc/dot_general | solution.py:55
  184.0 19.8 %scatter_fusion = f32[224,64,512]{2,1,0:T(8,128)} fusion(f32[224,64,512]{2,1,0:T(8,128)} %get-tuple-element.154, s32[64]{0:T(128)S(1)} %reshape.178, f32[64,64,512]{2,1,0:T(8,128)} %bitcast.90), kind=kCustom, calls=%fused_computation.1.clone.1 | custom fusion | flops 2097152 | bytes 25166080 | tf_op jit(solution)/shard_map/while/body/eval_jaxpr/scatter-add | solution.py:65
  224.4 14.8 %reshape.181 = f32[16,8,64,4,64]{4,3,2,1,0:T(4,128)} reshape(f32[16,8,64,256]{3,2,1,0:T(8,128)} %fusion.76) | data formatting | bytes 16777216 | tf_op jit(solution)/shard_map/while/body/eval_jaxpr/reshape | solution.py:51
  239.4 13.6 %fusion.77 = bf16[16,64,8,64]{3,2,1,0:T(8,128)(2,1)S(1)} fusion(f32[16,8,64,4,64]{4,3,2,1,0:T(4,128)} %reshape.181, s32[16,8,4]{2,1,0:T(8,128)S(1)} %copy.88), kind=kOutput, calls=%fused_computation.5.clone.1 | convolution fusion | flops 201854976 | bytes 9439232 | tf_op jit(solution)/shard_map/while/body/eval_jaxpr/ikms,ikamc->iasc/dot_general | solution.py:55
  260.9 19.7 %scatter_fusion = f32[224,64,512]{2,1,0:T(8,128)} fusion(f32[224,64,512]{2,1,0:T(8,128)} %get-tuple-element.154, s32[64]{0:T(128)S(1)} %reshape.178, f32[64,64,512]{2,1,0:T(8,128)} %bitcast.90), kind=kCustom, calls=%fused_computation.1.clone.1 | custom fusion | flops 2097152 | bytes 25166080 | tf_op jit(solution)/shard_map/while/body/eval_jaxpr/scatter-add | solution.py:65
  301.2 14.8 %reshape.181 = f32[16,8,64,4,64]{4,3,2,1,0:T(4,128)} reshape(f32[16,8,64,256]{3,2,1,0:T(8,128)} %fusion.76) | data formatting | bytes 16777216 | tf_op jit(solution)/shard_map/while/body/eval_jaxpr/reshape | solution.py:51
  316.2 13.6 %fusion.77 = bf16[16,64,8,64]{3,2,1,0:T(8,128)(2,1)S(1)} fusion(f32[16,8,64,4,64]{4,3,2,1,0:T(4,128)} %reshape.181, s32[16,8,4]{2,1,0:T(8,128)S(1)} %copy.88), kind=kOutput, calls=%fused_computation.5.clone.1 | convolution fusion | flops 201854976 | bytes 9439232 | tf_op jit(solution)/shard_map/while/body/eval_jaxpr/ikms,ikamc->iasc/dot_general | solution.py:55
  337.7 19.7 %scatter_fusion = f32[224,64,512]{2,1,0:T(8,128)} fusion(f32[224,64,512]{2,1,0:T(8,128)} %get-tuple-element.154, s32[64]{0:T(128)S(1)} %reshape.178, f32[64,64,512]{2,1,0:T(8,128)} %bitcast.90), kind=kCustom, calls=%fused_computation.1.clone.1 | custom fusion | flops 2097152 | bytes 25166080 | tf_op jit(solution)/shard_map/while/body/eval_jaxpr/scatter-add | solution.py:65
  378.0 14.8 %reshape.181 = f32[16,8,64,4,64]{4,3,2,1,0:T(4,128)} reshape(f32[16,8,64,256]{3,2,1,0:T(8,128)} %fusion.76) | data formatting | bytes 16777216 | tf_op jit(solution)/shard_map/while/body/eval_jaxpr/reshape | solution.py:51
  393.0 13.6 %fusion.77 = bf16[16,64,8,64]{3,2,1,0:T(8,128)(2,1)S(1)} fusion(f32[16,8,64,4,64]{4,3,2,1,0:T(4,128)} %reshape.181, s32[16,8,4]{2,1,0:T(8,128)S(1)} %copy.88), kind=kOutput, calls=%fused_computation.5.clone.1 | convolution fusion | flops 201854976 | bytes 9439232 | tf_op jit(solution)/shard_map/while/body/eval_jaxpr/ikms,ikamc->iasc/dot_general | solution.py:55
  414.4 19.6 %scatter_fusion = f32[224,64,512]{2,1,0:T(8,128)} fusion(f32[224,64,512]{2,1,0:T(8,128)} %get-tuple-element.154, s32[64]{0:T(128)S(1)} %reshape.178, f32[64,64,512]{2,1,0:T(8,128)} %bitcast.90), kind=kCustom, calls=%fused_computation.1.clone.1 | custom fusion | flops 2097152 | bytes 25166080 | tf_op jit(solution)/shard_map/while/body/eval_jaxpr/scatter-add | solution.py:65
  454.6 14.8 %reshape.181 = f32[16,8,64,4,64]{4,3,2,1,0:T(4,128)} reshape(f32[16,8,64,256]{3,2,1,0:T(8,128)} %fusion.76) | data formatting | bytes 16777216 | tf_op jit(solution)/shard_map/while/body/eval_jaxpr/reshape | solution.py:51
  469.7 13.6 %fusion.77 = bf16[16,64,8,64]{3,2,1,0:T(8,128)(2,1)S(1)} fusion(f32[16,8,64,4,64]{4,3,2,1,0:T(4,128)} %reshape.181, s32[16,8,4]{2,1,0:T(8,128)S(1)} %copy.88), kind=kOutput, calls=%fused_computation.5.clone.1 | convolution fusion | flops 201854976 | bytes 9439232 | tf_op jit(solution)/shard_map/while/body/eval_jaxpr/ikms,ikamc->iasc/dot_general | solution.py:55
  491.1 19.7 %scatter_fusion = f32[224,64,512]{2,1,0:T(8,128)} fusion(f32[224,64,512]{2,1,0:T(8,128)} %get-tuple-element.154, s32[64]{0:T(128)S(1)} %reshape.178, f32[64,64,512]{2,1,0:T(8,128)} %bitcast.90), kind=kCustom, calls=%fused_computation.1.clone.1 | custom fusion | flops 2097152 | bytes 25166080 | tf_op jit(solution)/shard_map/while/body/eval_jaxpr/scatter-add | solution.py:65
  531.4 14.8 %reshape.181 = f32[16,8,64,4,64]{4,3,2,1,0:T(4,128)} reshape(f32[16,8,64,256]{3,2,1,0:T(8,128)} %fusion.76) | data formatting | bytes 16777216 | tf_op jit(solution)/shard_map/while/body/eval_jaxpr/reshape | solution.py:51
  546.4 13.6 %fusion.77 = bf16[16,64,8,64]{3,2,1,0:T(8,128)(2,1)S(1)} fusion(f32[16,8,64,4,64]{4,3,2,1,0:T(4,128)} %reshape.181, s32[16,8,4]{2,1,0:T(8,128)S(1)} %copy.88), kind=kOutput, calls=%fused_computation.5.clone.1 | convolution fusion | flops 201854976 | bytes 9439232 | tf_op jit(solution)/shard_map/while/body/eval_jaxpr/ikms,ikamc->iasc/dot_general | solution.py:55
  567.9 19.8 %scatter_fusion = f32[224,64,512]{2,1,0:T(8,128)} fusion(f32[224,64,512]{2,1,0:T(8,128)} %get-tuple-element.154, s32[64]{0:T(128)S(1)} %reshape.178, f32[64,64,512]{2,1,0:T(8,128)} %bitcast.90), kind=kCustom, calls=%fused_computation.1.clone.1 | custom fusion | flops 2097152 | bytes 25166080 | tf_op jit(solution)/shard_map/while/body/eval_jaxpr/scatter-add | solution.py:65
  608.3 14.8 %reshape.181 = f32[16,8,64,4,64]{4,3,2,1,0:T(4,128)} reshape(f32[16,8,64,256]{3,2,1,0:T(8,128)} %fusion.76) | data formatting | bytes 16777216 | tf_op jit(solution)/shard_map/while/body/eval_jaxpr/reshape | solution.py:51
  623.3 13.6 %fusion.77 = bf16[16,64,8,64]{3,2,1,0:T(8,128)(2,1)S(1)} fusion(f32[16,8,64,4,64]{4,3,2,1,0:T(4,128)} %reshape.181, s32[16,8,4]{2,1,0:T(8,128)S(1)} %copy.88), kind=kOutput, calls=%fused_computation.5.clone.1 | convolution fusion | flops 201854976 | bytes 9439232 | tf_op jit(solution)/shard_map/while/body/eval_jaxpr/ikms,ikamc->iasc/dot_general | solution.py:55
  644.8 19.7 %scatter_fusion = f32[224,64,512]{2,1,0:T(8,128)} fusion(f32[224,64,512]{2,1,0:T(8,128)} %get-tuple-element.154, s32[64]{0:T(128)S(1)} %reshape.178, f32[64,64,512]{2,1,0:T(8,128)} %bitcast.90), kind=kCustom, calls=%fused_computation.1.clone.1 | custom fusion | flops 2097152 | bytes 25166080 | tf_op jit(solution)/shard_map/while/body/eval_jaxpr/scatter-add | solution.py:65
  664.7 10.8 %convert_element_type.31 = bf16[224,64,512]{2,1,0:T(8,128)(2,1)S(1)} convert(f32[224,64,512]{2,1,0:T(8,128)} %get-tuple-element.47) | non-fusion elementwise | flops 7340032 | bytes 44040192 | tf_op jit(solution)/shard_map/convert_element_type | solution.py:79
  675.5 8.5 %fusion.21 = bf16[28,64,512]{2,0,1:T(8,128)(2,1)S(1)} fusion(bf16[224,64,512]{2,1,0:T(8,128)(2,1)S(1)} %convert_element_type.31, s32[224]{0:T(256)S(1)} %copy-done, pred[224]{0:T(512)(128)(4,1)S(1)} %copy-done.6), kind=kOutput, calls=%fused_computation.30 | convolution fusion | flops 411971840 | bytes 16516192 | tf_op jit(solution)/shard_map/ct,tan->can/dot_general | solution.py:87
  695.9 36.2 %collective-permute-start.3 = (bf16[28,64,512]{2,1,0:T(8,128)(2,1)S(1)}, bf16[28,64,512]{2,1,0:T(8,128)(2,1)S(1)}, u32[]{:S(2)}, u32[]{:S(2)}) collective-permute-start(bf16[28,64,512]{2,1,0:T(8,128)(2,1)S(1)} %copy.48), channel_id=1, source_target_pairs={{0,1},{1,2},{2,3},{3,4},{4,5},{5,6},{6,7},{7,8},{8,9},{9,10},{10,1... | collective-permute-start | bytes 5505032 | tf_op jit(solution)/shard_map/ppermute | solution.py:31
  738.9 15.4 %fusion.12 = f32[8,64,512]{2,0,1:T(8,128)S(1)} fusion(bf16[224,64,512]{2,1,0:T(8,128)(2,1)S(1)} %convert_element_type.31, s32[224]{0:T(256)S(1)} %copy-done.7, pred[224]{0:T(512)(128)(4,1)S(1)} %copy-done.9), kind=kOutput, calls=%fused_computation.23 | convolution fusion | flops 117444096 | bytes 15729760 | tf_op jit(solution)/shard_map/rt,tan->ran/dot_general | solution.py:99
  757.5 46.8 %all-gather.2.cloned.1.call-done = bf16[32,64,512]{2,0,1:T(8,128)(2,1)} async-done(((bf16[8,64,512]{2,0,1:T(8,128)(2,1)}), bf16[32,64,512]{2,0,1:T(8,128)(2,1)}) %all-gather.2.cloned.1.call-update) | async-done | bytes 2097168 | tf_op jit(solution)/shard_map/all_gather | solution.py:108
  (203 shorter events, 272.9 us)
Async XLA Ops:
  6.5 14.9 %copy-start.10 = (s32[128,4]{0,1:T(4,128)S(1)}, s32[128,4]{0,1:T(4,128)}, u32[]{:S(2)}) copy-start(s32[128,4]{0,1:T(4,128)} %param.13) | copy-start | bytes 6148
  6.5 15.0 %copy-start.8 = (s32[128,8]{0,1:T(8,128)S(1)}, s32[128,8]{0,1:T(8,128)}, u32[]{:S(2)}) copy-start(s32[128,8]{0,1:T(8,128)} %param.10) | copy-start | bytes 12292
  6.5 15.1 %copy-start.2 = (s32[128,32]{0,1:T(8,128)S(1)}, s32[128,32]{0,1:T(8,128)}, u32[]{:S(2)}) copy-start(s32[128,32]{0,1:T(8,128)} %param.12) | copy-start | bytes 49156
  6.5 15.2 %copy-start.11 = (s32[224,1]{0,1:T(1,128)S(1)}, s32[224,1]{0,1:T(1,128)}, u32[]{:S(2)}) copy-start(s32[224,1]{0,1:T(1,128)} %param.14) | copy-start | bytes 2692
  6.5 797.7 %all-gather.2.cloned.1.call-start = ((), (), s32[]{:S(2)}) async-start(), calls=%async_computation | async-start | bytes 2621440 | tf_op jit(solution)/shard_map/all_gather | solution.py:108
  6.6 18.2 %collective-permute-start.1 = (bf16[128,64,256]{2,1,0:T(8,128)(2,1)}, bf16[128,64,256]{2,1,0:T(8,128)(2,1)}, u32[]{:S(2)}, u32[]{:S(2)}) collective-permute-start(bf16[128,64,256]{2,1,0:T(8,128)(2,1)} %param.11), channel_id=1, source_target_pairs={{1,0},{2,1},{3,2},{4,3},{5,4},{6,5},{7,6},{8,7},{9,8},{10,9},{11,1... | collective-permute-start | bytes 12582920 | tf_op jit(solution)/shard_map/ppermute | solution.py:23
  8.0 16.7 %collective-permute-start = (bf16[128,64,256]{2,1,0:T(8,128)(2,1)}, bf16[128,64,256]{2,1,0:T(8,128)(2,1)}, u32[]{:S(2)}, u32[]{:S(2)}) collective-permute-start(bf16[128,64,256]{2,1,0:T(8,128)(2,1)} %param.11), channel_id=1, source_target_pairs={{0,1},{1,2},{2,3},{3,4},{4,5},{5,6},{6,7},{7,8},{8,9},{9,10},{10,1... | collective-permute-start | bytes 12582920 | tf_op jit(solution)/shard_map/ppermute | solution.py:22
  22.2 0.6 copy-start.3
  22.2 14.1 %copy-start.5 = (pred[224]{0:T(512)(128)(4,1)}, pred[224]{0:T(512)(128)(4,1)S(1)}, u32[]{:S(2)}) copy-start(pred[224]{0:T(512)(128)(4,1)S(1)} %get-tuple-element.76) | copy-start | bytes 676
  664.6 10.8 %copy-start = (s32[224]{0:T(256)S(1)}, s32[224]{0:T(256)}, u32[]{:S(2)}) copy-start(s32[224]{0:T(256)} %slice_add_fusion) | copy-start | bytes 2692
  664.7 10.8 %copy-start.6 = (pred[224]{0:T(512)(128)(4,1)S(1)}, pred[224]{0:T(512)(128)(4,1)}, u32[]{:S(2)}) copy-start(pred[224]{0:T(512)(128)(4,1)} %copy-done.5) | copy-start | bytes 676
  675.5 10.9 %copy-start.1 = (s32[224]{0:T(256)S(1)}, s32[224]{0:T(256)}, u32[]{:S(2)}) copy-start(s32[224]{0:T(256)} %slice_add_fusion.1) | copy-start | bytes 2692
  675.5 10.9 %copy-start.4 = (pred[224]{0:T(512)(128)(4,1)S(1)}, pred[224]{0:T(512)(128)(4,1)}, u32[]{:S(2)}) copy-start(pred[224]{0:T(512)(128)(4,1)} %copy-done.3) | copy-start | bytes 676
  685.0 47.2 %copy-start.7 = (s32[224]{0:T(256)S(1)}, s32[224]{0:T(256)}, u32[]{:S(2)}) copy-start(s32[224]{0:T(256)} %param.15) | copy-start | bytes 2692
  685.0 53.9 %copy-start.9 = (pred[224]{0:T(512)(128)(4,1)S(1)}, pred[224]{0:T(512)(128)(4,1)}, u32[]{:S(2)}) copy-start(pred[224]{0:T(512)(128)(4,1)} %get-tuple-element.75) | copy-start | bytes 676
  685.1 69.3 %collective-permute-start.5 = (bf16[28,64,512]{2,1,0:T(8,128)(2,1)S(1)}, bf16[28,64,512]{2,1,0:T(8,128)(2,1)S(1)}, u32[]{:S(2)}, u32[]{:S(2)}) collective-permute-start(bf16[28,64,512]{2,1,0:T(8,128)(2,1)S(1)} %copy.51), channel_id=1, source_target_pairs={{1,0},{2,1},{3,2},{4,3},{5,4},{6,5},{7,6},{8,7},{9,8},{10,9},{11,1... | collective-permute-start | bytes 5505032 | tf_op jit(solution)/shard_map/ppermute | solution.py:31
  695.9 59.6 %collective-permute-start.3 = (bf16[28,64,512]{2,1,0:T(8,128)(2,1)S(1)}, bf16[28,64,512]{2,1,0:T(8,128)(2,1)S(1)}, u32[]{:S(2)}, u32[]{:S(2)}) collective-permute-start(bf16[28,64,512]{2,1,0:T(8,128)(2,1)S(1)} %copy.48), channel_id=1, source_target_pairs={{0,1},{1,2},{2,3},{3,4},{4,5},{5,6},{6,7},{7,8},{8,9},{9,10},{10,1... | collective-permute-start | bytes 5505032 | tf_op jit(solution)/shard_map/ppermute | solution.py:31
  732.4 22.0 %collective-permute-start.4 = (s32[28]{0:T(128)S(1)}, s32[28]{0:T(128)S(1)}, u32[]{:S(2)}, u32[]{:S(2)}) collective-permute-start(s32[28]{0:T(128)S(1)} %broadcast_select_fusion), channel_id=1, source_target_pairs={{1,0},{2,1},{3,2},{4,3},{5,4},{6,5},{7,6},{8,7},{9,8},{10,9},{11,1... | collective-permute-start | bytes 344 | tf_op jit(solution)/shard_map/ppermute | solution.py:31
  733.7 21.8 %collective-permute-start.2 = (s32[28]{0:T(128)S(1)}, s32[28]{0:T(128)S(1)}, u32[]{:S(2)}, u32[]{:S(2)}) collective-permute-start(s32[28]{0:T(128)S(1)} %broadcast_select_fusion.1), channel_id=1, source_target_pairs={{0,1},{1,2},{2,3},{3,4},{4,5},{5,6},{6,7},{7,8},{8,9},{9,10},{10,1... | collective-permute-start | bytes 344 | tf_op jit(solution)/shard_map/ppermute | solution.py:31
Sparse Core Ops, SparseCore 0:
  757.6 46.6 all-gather.1
where the time goes:
time: 825 us; the launch traced here: 815 us
  local copies, waits for them, and re-layouts  277 us (34%)
  matrix products  243 us (29%)
  other arithmetic  183 us (22%)
  starting transfers between devices  50.5 us (6%)
  waiting for transfers between devices  46.8 us (6%)
  between operations  13.8 us (2%)
    scatter-add x8, other arithmetic, add_block(): jax.ops.segment_sum(pieces.reshape(block_rows * KP, BS, KC * BS), touch_p...  158 us
    reshape x8, local copies, waits for them, and re-layouts, add_block(): products = products.reshape(block_rows, KA, BS, KP, BS)  118 us
    dot_general x8, matrix products, add_block(): jnp.einsum('ikms,ikamc->iasc', onehot, products, precision=lax.Precision....  109 us
    gather x8, local copies, waits for them, and re-layouts, add_block(): nearby = window[col_part]  58.7 us
    dot_general x8, matrix products, add_block(): jnp.einsum('iakb,ikbn->ikan', a_part.reshape(block_rows, BS, KA, BS), nea...  52.8 us
    all_gather x1, waiting for transfers between devices, on_device(): return lax.all_gather(owned, 'grp', axis=0, tiled=True)  46.8 us
    dot_general x8, matrix products, add_block(): jnp.einsum('iamb,ian->imbn', p_part.reshape(block_rows, BS, KP, BS), roun...  46.3 us
    ppermute x4, starting transfers between devices, shifted(): return lax.ppermute(value, axis, pairs)  44 us
  transfers between devices with their start and end apart: 7, of which 1 were waited for; matrix products, arithmetic and copies ran while one was open for 5% of the time, Pallas kernels for 0%

commit v1 on v0

v1 whole, which is shorter than its diff:
```python
import functools

import jax
import jax.numpy as jnp
from jax import lax
from jax.experimental import pallas as pl
from jax.experimental.pallas import tpu as pltpu
from jax.sharding import PartitionSpec as P

BS = 64
KA = 8
KP = 4
KC = 8
CB = 8
NT = 224
FB = 128
HALO = 32
SUBSETS = 1 << KP
WINDOW = FB + 2 * HALO
P_ROWS = 16
LOCAL_STEPS = FB // P_ROWS
HALO_STEPS = HALO // P_ROWS
BUILD_STEPS = LOCAL_STEPS + 2 * HALO_STEPS
GROUP = 8
UNROLL = 4
MAIN_STEPS = FB // GROUP
TARGETS = 3 * CB
MESH = pl.DeviceIdType.MESH


def build_rows(source, base, table, left):
    def row(r, carry):
        p = source[r].astype(jnp.float32)
        single = []
        for pair in range(KP // 2):
            tile = p[:, pair * 128:(pair + 1) * 128]
            turned = pltpu.roll(tile, 64, 1)
            single.append(jnp.where(left, tile, turned))
            single.append(jnp.where(left, turned, tile))
        sums = {0: None}
        at = (base + r) * SUBSETS
        for subset in range(1, SUBSETS):
            low = subset & -subset
            rest = subset ^ low
            value = single[low.bit_length() - 1]
            if rest:
                value = value + sums[rest]
            sums[subset] = value
            table[at + subset] = value.astype(jnp.bfloat16)
        return carry

    lax.fori_loop(0, P_ROWS, row, 0)


def galerkin_kernel(codes, touch, targets, p_local, p_prev, p_next, a_ref, p_ref, own_ref, prev_ref,
                    next_ref, table, acc):
    step = pl.program_id(0)
    left = lax.broadcasted_iota(jnp.int32, (BS, 128), 1) < 64

    @pl.when(step == 0)
    def _():
        table[0] = jnp.zeros((BS, 128), jnp.bfloat16)
        acc[...] = jnp.zeros_like(acc)

    @pl.when(step < LOCAL_STEPS)
    def _():
        build_rows(p_local, step * P_ROWS, table, left)

    @pl.when((step >= LOCAL_STEPS) & (step < LOCAL_STEPS + HALO_STEPS))
    def _():
        build_rows(p_prev, step * P_ROWS, table, left)

    @pl.when((step >= LOCAL_STEPS + HALO_STEPS) & (step < BUILD_STEPS))
    def _():
        build_rows(p_next, step * P_ROWS, table, left)

    @pl.when(step >= BUILD_STEPS)
    def _():
        first = (step - BUILD_STEPS) * GROUP

        def rows(it, carry):
            for u in range(UNROLL):
                r = it * UNROLL + u
                i = first + r
                halves = []
                for nt in range(2):
                    total = None
                    for kt in range(2):
                        blocks = []
                        for k in range(4 * kt, 4 * kt + 4):
                            tiles = []
                            for s in range(4 * nt, 4 * nt + 4, 2):
                                at = i * (KA * KC) + k * KC + s
                                tiles.append(jnp.where(left, table[codes[at]], table[codes[at + 1]]))
                            blocks.append(jnp.concatenate(tiles, axis=1))
                        part = jnp.dot(a_ref[r, :, kt * 256:(kt + 1) * 256],
                                       jnp.concatenate(blocks, axis=0),
                                       preferred_element_type=jnp.float32)
                        total = part if total is None else total + part
                    halves.append(total.astype(jnp.bfloat16))
                rounded = jnp.concatenate(halves, axis=1)
                pieces = lax.dot_general(p_ref[r], rounded, (((0,), (0,)), ((), ())),
                                         preferred_element_type=jnp.float32)
                for m in range(KP):
                    to = targets[touch[i * KP + m]]
                    acc[to] += pieces[m * BS:(m + 1) * BS]
            return carry

        lax.fori_loop(0, GROUP // UNROLL, rows, 0)

    @pl.when(step == BUILD_STEPS + MAIN_STEPS - 1)
    def _():
        prev_ref[...] = acc[0:CB].astype(jnp.bfloat16)
        own_ref[...] = acc[CB:2 * CB]
        next_ref[...] = acc[2 * CB:3 * CB].astype(jnp.bfloat16)


def galerkin(codes, touch, targets, p_local, p_prev, p_next, a_blocks):
    def clamp(value, top):
        return jnp.clip(value, 0, top)

    def main(step):
        return clamp(step - BUILD_STEPS, MAIN_STEPS - 1)

    whole = lambda s, *_: (0, 0, 0)
    p_shape = (P_ROWS, BS, KP * BS)
    grid_spec = pltpu.PrefetchScalarGridSpec(
        num_scalar_prefetch=3,
        grid=(BUILD_STEPS + MAIN_STEPS,),
        in_specs=[
            pl.BlockSpec(p_shape, lambda s, *_: (clamp(s, LOCAL_STEPS - 1), 0, 0)),
            pl.BlockSpec(p_shape, lambda s, *_: (clamp(s - LOCAL_STEPS, HALO_STEPS - 1), 0, 0)),
            pl.BlockSpec(p_shape, lambda s, *_: (clamp(s - LOCAL_STEPS - HALO_STEPS, HALO_STEPS - 1), 0, 0)),
            pl.BlockSpec((GROUP, BS, KA * BS), lambda s, *_: (main(s), 0, 0)),
            pl.BlockSpec((GROUP, BS, KP * BS), lambda s, *_: (main(s), 0, 0)),
        ],
        out_specs=[pl.BlockSpec((CB, BS, KC * BS), whole)] * 3,
        scratch_shapes=[
            pltpu.VMEM((WINDOW * SUBSETS, BS, 128), jnp.bfloat16),
            pltpu.VMEM((TARGETS, BS, KC * BS), jnp.float32),
        ],
    )
    rows = (CB, BS, KC * BS)
    return pl.pallas_call(
        galerkin_kernel,
        grid_spec=grid_spec,
        out_shape=[
            jax.ShapeDtypeStruct(rows, jnp.float32),
            jax.ShapeDtypeStruct(rows, jnp.bfloat16),
            jax.ShapeDtypeStruct(rows, jnp.bfloat16),
        ],
        compiler_params=pltpu.CompilerParams(vmem_limit_bytes=62 * 1024 * 1024),
        cost_estimate=pl.CostEstimate(flops=8_600_000_000, bytes_accessed=20_000_000, transcendentals=0),
    )(codes, touch, targets, p_local, p_prev, p_next, a_blocks, p_local)


def exchange_kernel(n_grp, n_dev, own_ref, prev_ref, next_ref, out_ref, from_prev, from_next, sems_out,
                    sems_in):
    g = lax.axis_index("grp")
    d = lax.axis_index("dev")
    count = n_grp * n_dev
    position = g * n_dev + d
    after = lax.rem(position + 1, count)
    before = lax.rem(position + count - 1, count)
    after_id = (after // n_dev, lax.rem(after, n_dev))
    before_id = (before // n_dev, lax.rem(before, n_dev))
    up_id = (lax.rem(g + 1, n_grp), d)
    down_id = (lax.rem(g + n_grp - 1, n_grp), d)

    barrier = pltpu.get_barrier_semaphore()
    for other in (after_id, before_id, up_id, down_id):
        pl.semaphore_signal(barrier, inc=1, device_id=other, device_id_type=MESH)
    pl.semaphore_wait(barrier, 4)

    def copy(source, target, kind, r, device):
        return pltpu.make_async_remote_copy(
            src_ref=source, dst_ref=target, send_sem=sems_out.at[kind, r], recv_sem=sems_in.at[kind, r],
            device_id=device, device_id_type=MESH)

    sent = []
    to_after = [copy(next_ref.at[r], from_prev.at[r], 0, r, after_id) for r in range(CB)]
    to_before = [copy(prev_ref.at[r], from_next.at[r], 1, r, before_id) for r in range(CB)]
    for r in range(CB):
        to_after[r].start()
        to_before[r].start()
    below = lax.rem(g + n_grp - 1, n_grp)
    above = lax.rem(g + 1, n_grp)
    ups, downs, relays = [], [], []

    def relay(r):
        if r < CB // 2:
            ups[r].wait_recv()
            block = below * CB + r
            onward = copy(out_ref.at[block], out_ref.at[block], 4, r, up_id)
        else:
            downs[r].wait_recv()
            block = above * CB + r
            onward = copy(out_ref.at[block], out_ref.at[block], 4, r, down_id)
        onward.start()
        relays.append(onward)

    for r in range(CB):
        to_after[r].wait_recv()
        to_before[r].wait_recv()
        total = own_ref[r] + from_prev[r].astype(jnp.float32) + from_next[r].astype(jnp.float32)
        block = g * CB + r
        out_ref[block] = total.astype(jnp.bfloat16)
        up = copy(out_ref.at[block], out_ref.at[block], 2, r, up_id)
        down = copy(out_ref.at[block], out_ref.at[block], 3, r, down_id)
        up.start()
        down.start()
        ups.append(up)
        downs.append(down)
        if r >= 1:
            relay(r - 1)
    relay(CB - 1)
    for r in range(CB):
        if r < CB // 2:
            downs[r].wait_recv()
        else:
            ups[r].wait_recv()
        relays[r].wait_recv()
        for c in (to_after[r], to_before[r], ups[r], downs[r], relays[r]):
            c.wait_send()


def exchange(own, to_prev, to_next):
    n_grp, n_dev = lax.axis_size("grp"), lax.axis_size("dev")
    rows = (CB, BS, KC * BS)
    return pl.pallas_call(
        functools.partial(exchange_kernel, n_grp, n_dev),
        out_shape=jax.ShapeDtypeStruct((n_grp * CB, BS, KC * BS), jnp.bfloat16),
        in_specs=[pl.BlockSpec(memory_space=pltpu.VMEM)] * 3,
        out_specs=pl.BlockSpec(memory_space=pltpu.VMEM),
        scratch_shapes=[
            pltpu.VMEM(rows, jnp.bfloat16),
            pltpu.VMEM(rows, jnp.bfloat16),
            pltpu.SemaphoreType.DMA((5, CB)),
            pltpu.SemaphoreType.DMA((5, CB)),
        ],
        compiler_params=pltpu.CompilerParams(collective_id=0, has_side_effects=True,
                                             vmem_limit_bytes=32 * 1024 * 1024),
    )(own, to_prev, to_next)


def on_device(a_blocks, a_cols, p_blocks, ap_slots, p_touch, owner_dev, owner_row):
    axes = ("grp", "dev")
    position = lax.axis_index(axes)
    count = lax.axis_size(axes)
    up = [(i, (i + 1) % count) for i in range(count)]
    down = [(j, i) for i, j in up]
    p_prev = lax.ppermute(p_blocks[FB - HALO:], axes, up)
    p_next = lax.ppermute(p_blocks[:HALO], axes, down)

    local = a_cols - position * FB
    window = jnp.where(local < 0, local + HALO + FB, jnp.where(local >= FB, local + HALO, local))
    slots = ap_slots.reshape(FB, KA, KP)
    weights = jnp.int32(1) << jnp.arange(KP, dtype=jnp.int32)
    hits = slots[:, :, :, None] == jnp.arange(KC, dtype=jnp.int32)
    subset = jnp.sum(jnp.where(hits, weights[:, None], 0), axis=2)
    codes = jnp.where(subset == 0, 0, window[:, :, None] * SUBSETS + subset)
    targets = (owner_dev[:, 0] - position + 1) * CB + owner_row
    own, to_prev, to_next = galerkin(codes.reshape(-1), p_touch.reshape(-1), targets, p_blocks, p_prev, p_next,
                                     a_blocks)
    return exchange(own, to_prev, to_next)


def solution(mesh):
    placed = (
        P(("grp", "dev"), None, None),
        P(("grp", "dev"), None),
        P(("grp", "dev"), None, None),
        P(("grp", "dev"), None),
        P(("grp", "dev"), None),
        P(("grp", "dev"), None),
        P(("grp", "dev")),
    )
    return jax.shard_map(
        on_device, mesh=mesh, in_specs=placed, out_specs=P("dev", None, None), check_vma=False
    )
```

time: 825 us -> 137 us (0.17)
  local copies, waits for them, and re-layouts: 277 us -> 8.25 us
  matrix products: 243 us -> 0 us
  other arithmetic: 183 us -> 0.66 us
  Pallas kernels: 0 us -> 101 us
  starting transfers between devices: 50.5 us -> 8.28 us
  waiting for transfers between devices: 46.8 us -> 17.2 us
  between operations: 13.8 us -> 0.06 us
    dot_general x29 -> x0, matrix products: 243 us -> none  [the longest x8 109 us: add_block(): jnp.einsum('ikms,ikamc->iasc', onehot, products, precision=lax.Precision....]
    scatter-add x8 -> x0, other arithmetic: 158 us -> none  [add_block(): jax.ops.segment_sum(pieces.reshape(block_rows * KP, BS, KC * BS), touch_p...]
    reshape x25 -> x1, local copies, waits for them, and re-layouts: 141 us -> 0.68 us  [on_device(): p_touch.reshape(-1)]
    pallas_call x0 -> x2, Pallas kernels: none -> 101 us  [the longest x1 68.1 us: galerkin(): pl.pallas_call(galerkin_kernel, grid_spec=grid_spec, out_shape=[jax.Shape...]
    gather x8 -> x0, local copies, waits for them, and re-layouts: 58.7 us -> none  [add_block(): nearby = window[col_part]]
    all_gather x1 -> x0, waiting for transfers between devices: 46.8 us -> none  [on_device(): return lax.all_gather(owned, 'grp', axis=0, tiled=True)]
    ppermute x6 -> x2, starting transfers between devices: 50.4 us -> 8.28 us  [the longest x1 8.27 us: on_device(): p_next = lax.ppermute(p_blocks[:HALO], axes, down)]
    dynamic_slice x48 -> x0, local copies, waits for them, and re-layouts: 29.4 us -> none  [on_device(): summed, _ = lax.scan(add_block, start, inputs)]
  transfers between devices with their start and end apart: 7 -> 2, of which waited for: 1 -> 2; matrix products, arithmetic and copies ran while one was open for 5% -> 2% of each run, Pallas kernels for 0% -> 0%
where the time goes in v1:
time: 137 us; the launch traced here: 135 us
  Pallas kernels  101 us (74%)
  waiting for transfers between devices  17.2 us (13%)
  starting transfers between devices  8.28 us (6%)
  local copies, waits for them, and re-layouts  8.25 us (6%)
    pallas_call x1, Pallas kernels, galerkin(): pl.pallas_call(galerkin_kernel, grid_spec=grid_spec, out_shape=[jax.Shape...  68.1 us
    pallas_call x1, Pallas kernels, exchange(): pl.pallas_call(functools.partial(exchange_kernel, n_grp, n_dev), out_shap...  32.6 us
    ppermute x1, waiting for transfers between devices, on_device(): p_next = lax.ppermute(p_blocks[:HALO], axes, down)  9.74 us
    ppermute x1, starting transfers between devices, on_device(): p_next = lax.ppermute(p_blocks[:HALO], axes, down)  8.27 us
    ppermute x1, waiting for transfers between devices, on_device(): p_prev = lax.ppermute(p_blocks[FB - HALO:], axes, up)  7.44 us
    unnamed x18, local copies, waits for them, and re-layouts  4.76 us
  transfers between devices with their start and end apart: 2, of which 2 were waited for; matrix products, arithmetic and copies ran while one was open for 2% of the time, Pallas kernels for 0%

profile of v1, /device:TPU:0, one launch (start us, length us, event | category | flops | bytes accessed | tf_op | source)
XLA Modules:
  0.0 135.2 jit_solution(4460625340717498304)
XLA Ops:
  0.0 0.0 copy-start.5
  0.0 0.0 copy-start.3
  0.0 0.0 copy-start.4
  0.0 0.0 copy-start.7
  0.0 0.0 copy-start.6
  0.0 1.7 %fusion.2 = (bf16[32,64,256]{2,1,0:T(8,128)(2,1)S(1)}, bf16[32,64,256]{2,1,0:T(8,128)(2,1)S(1)}) fusion(bf16[128,64,256]{2,1,0:T(8,128)(2,1)} %p_ref.1), kind=kLoop, calls=%fused_computation.8 | loop fusion | bytes 4194304 | tf_op jit(solution)/shard_map/slice | solution.py:253
  1.8 8.3 %collective-permute-start.1 = (bf16[32,64,256]{2,1,0:T(8,128)(2,1)S(1)}, bf16[32,64,256]{2,1,0:T(8,128)(2,1)}, u32[]{:S(2)}, u32[]{:S(2)}) collective-permute-start(bf16[32,64,256]{2,1,0:T(8,128)(2,1)S(1)} %get-tuple-element.11), channel_id=1, source_target_pairs={{1,0},{2,1},{3,2},{4,3},{5,4},{6,5},{7,6},{8,7},{9,8},{10,9},{11,1... | collective-permute-start | bytes 3145736 | tf_op jit(solution)/shard_map/ppermute | solution.py:253
  10.0 0.0 collective-permute-start
  10.0 0.0 copy-done.5
  10.0 0.1 copy.14
  10.2 0.7 reshape.20.touch
  10.8 0.0 copy-done.3
  10.8 0.1 select_reduce_fusion
  10.9 0.0 copy-done.4
  11.0 0.2 copy.13
  11.2 0.8 select_n.23.codes
  12.0 0.0 copy-done.7
  12.1 0.0 copy-done.6
  12.1 0.5 add.42.targets
  12.6 9.7 %collective-permute-done.1.p_next = bf16[32,64,256]{2,1,0:T(8,128)(2,1)} collective-permute-done((bf16[32,64,256]{2,1,0:T(8,128)(2,1)S(1)}, bf16[32,64,256]{2,1,0:T(8,128)(2,1)}, u32[]{:S(2)}, u32[]{:S(2)}) %collective-permute-start.1) | collective-permute-done | bytes 1048608 | tf_op jit(solution)/shard_map/ppermute | solution.py:253
  22.4 7.4 %collective-permute-done.p_prev = bf16[32,64,256]{2,1,0:T(8,128)(2,1)} collective-permute-done((bf16[32,64,256]{2,1,0:T(8,128)(2,1)S(1)}, bf16[32,64,256]{2,1,0:T(8,128)(2,1)}, u32[]{:S(2)}, u32[]{:S(2)}) %collective-permute-start) | collective-permute-done | bytes 1048608 | tf_op jit(solution)/shard_map/ppermute | solution.py:252
  29.8 68.1 %shard_map.73 = (f32[8,64,512]{2,1,0:T(8,128)}, bf16[8,64,512]{2,1,0:T(8,128)(2,1)}, bf16[8,64,512]{2,1,0:T(8,128)(2,1)}) custom-call(s32[8192]{0:T(1024)} %select_n.23.codes, s32[512]{0:T(512)} %reshape.20.touch, s32[224]{0:T(256)} %add.42.targets, bf16[128,64,256]{2,1,0:T(8,128)(2,1)} %p_ref.1, bf16[32,64,256]{2,1,0:T(8,128)(2,1)} %collective-permute-done.p_prev, ...), custom_call_target="tpu_custom_call" | custom-call | flops 8600000512 | bytes 20000000 | tf_op jit(solution)/shard_map/pallas_call | solution.py:144
  97.9 0.0 copy-start
  97.9 1.2 copy-done
  99.1 0.0 copy-start.1
  99.2 1.0 copy-done.1
  100.2 0.0 copy-start.2
  100.2 1.0 copy-done.2
  101.2 32.6 %shard_map.74 = bf16[32,64,512]{2,1,0:T(8,128)(2,1)S(1)} custom-call(f32[8,64,512]{2,1,0:T(8,128)S(1)} %copy-done, bf16[8,64,512]{2,1,0:T(8,128)(2,1)S(1)} %copy-done.1, bf16[8,64,512]{2,1,0:T(8,128)(2,1)S(1)} %copy-done.2), custom_call_target="tpu_custom_call" | custom-call | tf_op jit(solution)/shard_map/pallas_call | solution.py:230
  133.9 1.3 copy.16
  (4 shorter events, 0.0 us)
Async XLA Ops:
  0.0 10.0 %copy-start.5 = (s32[128,4]{0,1:T(4,128)S(1)}, s32[128,4]{0,1:T(4,128)}, u32[]{:S(2)}) copy-start(s32[128,4]{0,1:T(4,128)} %param.11) | copy-start | bytes 6148
  0.0 10.8 %copy-start.3 = (s32[128,32]{0,1:T(8,128)S(1)}, s32[128,32]{0,1:T(8,128)}, u32[]{:S(2)}) copy-start(s32[128,32]{0,1:T(8,128)} %param.10) | copy-start | bytes 49156
  0.0 10.9 %copy-start.4 = (s32[128,8]{0,1:T(8,128)S(1)}, s32[128,8]{0,1:T(8,128)}, u32[]{:S(2)}) copy-start(s32[128,8]{0,1:T(8,128)} %param.8) | copy-start | bytes 12292
  0.0 12.0 %copy-start.7 = (s32[224,1]{0,1:T(1,128)S(1)}, s32[224,1]{0,1:T(1,128)}, u32[]{:S(2)}) copy-start(s32[224,1]{0,1:T(1,128)} %param.12) | copy-start | bytes 2692
  0.0 12.1 %copy-start.6 = (s32[224]{0:T(256)S(1)}, s32[224]{0:T(256)}, u32[]{:S(2)}) copy-start(s32[224]{0:T(256)} %param.13) | copy-start | bytes 2692
  1.8 20.6 %collective-permute-start.1 = (bf16[32,64,256]{2,1,0:T(8,128)(2,1)S(1)}, bf16[32,64,256]{2,1,0:T(8,128)(2,1)}, u32[]{:S(2)}, u32[]{:S(2)}) collective-permute-start(bf16[32,64,256]{2,1,0:T(8,128)(2,1)S(1)} %get-tuple-element.11), channel_id=1, source_target_pairs={{1,0},{2,1},{3,2},{4,3},{5,4},{6,5},{7,6},{8,7},{9,8},{10,9},{11,1... | collective-permute-start | bytes 3145736 | tf_op jit(solution)/shard_map/ppermute | solution.py:253
  10.0 19.8 %collective-permute-start = (bf16[32,64,256]{2,1,0:T(8,128)(2,1)S(1)}, bf16[32,64,256]{2,1,0:T(8,128)(2,1)}, u32[]{:S(2)}, u32[]{:S(2)}) collective-permute-start(bf16[32,64,256]{2,1,0:T(8,128)(2,1)S(1)} %get-tuple-element.12), channel_id=1, source_target_pairs={{0,1},{1,2},{2,3},{3,4},{4,5},{5,6},{6,7},{7,8},{8,9},{9,10},{10,1... | collective-permute-start | bytes 3145736 | tf_op jit(solution)/shard_map/ppermute | solution.py:252
  97.9 1.2 copy-start
  99.1 1.0 copy-start.1
  100.2 1.0 copy-start.2

commit v2 on v1

v2 whole, which is shorter than its diff:
```python
import functools

import jax
import jax.numpy as jnp
from jax import lax
from jax.experimental import pallas as pl
from jax.experimental.pallas import tpu as pltpu
from jax.sharding import PartitionSpec as P

BS = 64
KA = 8
KP = 4
KC = 8
CB = 8
NT = 224
FB = 128
HALO = 32
SUBSETS = 1 << KP
P_ROWS = 32
LOCAL_STEPS = FB // P_ROWS
GROUP = 16
UNROLL = 8
MAIN_STEPS = FB // GROUP
TARGETS = 3 * CB
MESH = pl.DeviceIdType.MESH


def build_rows(source, base, table, left):
    def row(r, carry):
        p = source[r].astype(jnp.float32)
        single = []
        for pair in range(KP // 2):
            tile = p[:, pair * 128:(pair + 1) * 128]
            turned = pltpu.roll(tile, 64, 1)
            single.append(jnp.where(left, tile, turned))
            single.append(jnp.where(left, turned, tile))
        sums = {0: None}
        at = (base + r) * SUBSETS
        for subset in range(1, SUBSETS):
            low = subset & -subset
            rest = subset ^ low
            value = single[low.bit_length() - 1]
            if rest:
                value = value + sums[rest]
            sums[subset] = value
            table[at + subset] = value.astype(jnp.bfloat16)
        return carry

    lax.fori_loop(0, P_ROWS, row, 0, unroll=4)


def left_half():
    return lax.broadcasted_iota(jnp.int32, (BS, 128), 1) < 64


def coefficients(table, codes, first, blocks, nt, left):
    rows = []
    for k in range(blocks):
        tiles = []
        for s in range(4 * nt, 4 * nt + 4, 2):
            at = first + k * KC + s
            tiles.append(jnp.where(left, table[codes[at]], table[codes[at + 1]]))
        rows.append(jnp.concatenate(tiles, axis=1))
    return jnp.concatenate(rows, axis=0)


def local_kernel(codes, edge, p_ref, a_ref, out_ref, table):
    step = pl.program_id(0)
    left = left_half()

    @pl.when(step == 0)
    def _():
        table[0] = jnp.zeros((BS, 128), jnp.bfloat16)

    @pl.when(step < LOCAL_STEPS)
    def _():
        build_rows(p_ref, step * P_ROWS, table, left)

    def assemble(cuts):
        first = (step - LOCAL_STEPS) * GROUP

        def rows(it, carry):
            for u in range(UNROLL):
                r = it * UNROLL + u
                for nt in range(2):
                    total = None
                    for low, high in cuts:
                        weights = coefficients(table, codes, (first + r) * (KA * KC) + low * KC, high - low, nt, left)
                        part = jnp.dot(a_ref[r, :, low * BS:high * BS], weights,
                                       preferred_element_type=jnp.float32)
                        total = part if total is None else total + part
                    out_ref[r, :, nt * 256:(nt + 1) * 256] = total.astype(jnp.bfloat16)
            return carry

        lax.fori_loop(0, GROUP // UNROLL, rows, 0)

    @pl.when((step >= LOCAL_STEPS) & (edge[0] == 0))
    def _():
        assemble(((0, 4), (4, KA - 2)))

    @pl.when((step >= LOCAL_STEPS) & (edge[0] != 0))
    def _():
        assemble(((0, 4), (4, KA)))


def local_part(codes, edge, p_local, a_blocks):
    main = lambda s, *_: (jnp.maximum(s - LOCAL_STEPS, 0), 0, 0)
    return pl.pallas_call(
        local_kernel,
        grid_spec=pltpu.PrefetchScalarGridSpec(
            num_scalar_prefetch=2,
            grid=(LOCAL_STEPS + MAIN_STEPS,),
            in_specs=[
                pl.BlockSpec((P_ROWS, BS, KP * BS), lambda s, *_: (jnp.minimum(s, LOCAL_STEPS - 1), 0, 0)),
                pl.BlockSpec((GROUP, BS, KA * BS), main),
            ],
            out_specs=pl.BlockSpec((GROUP, BS, KC * BS), main),
            scratch_shapes=[pltpu.VMEM((FB * SUBSETS, BS, 128), jnp.bfloat16)],
        ),
        out_shape=jax.ShapeDtypeStruct((FB, BS, KC * BS), jnp.bfloat16),
        compiler_params=pltpu.CompilerParams(vmem_limit_bytes=44 * 1024 * 1024),
        cost_estimate=pl.CostEstimate(flops=16_000_000_000, bytes_accessed=20_000_000, transcendentals=0),
    )(codes, edge, p_local, a_blocks)


def halo_kernel(codes, touch, targets, p_prev, p_next, part_ref, a_ref, p_ref, own_ref, prev_ref, next_ref,
                table, acc):
    step = pl.program_id(0)
    left = left_half()

    @pl.when(step == 0)
    def _():
        acc[...] = jnp.zeros_like(acc)
        build_rows(p_prev, 0, table, left)
        build_rows(p_next, HALO, table, left)
        table[0] = jnp.zeros((BS, 128), jnp.bfloat16)

    def rows(it, carry):
        kept = []
        for u in range(UNROLL + 1):
            if u < UNROLL:
                r = it * UNROLL + u
                i = step * GROUP + r
                halves = []
                for nt in range(2):
                    weights = coefficients(table, codes, i * (2 * KC), 2, nt, left)
                    total = jnp.dot(a_ref[r], weights, preferred_element_type=jnp.float32)
                    total = total + part_ref[r, :, nt * 256:(nt + 1) * 256].astype(jnp.float32)
                    halves.append(total.astype(jnp.bfloat16))
                kept.append(jnp.concatenate(halves, axis=1))
            if u >= 1:
                r = it * UNROLL + u - 1
                i = step * GROUP + r
                pieces = lax.dot_general(p_ref[r], kept[u - 1], (((0,), (0,)), ((), ())),
                                         preferred_element_type=jnp.float32)
                for m in range(KP):
                    to = targets[touch[i * KP + m]]
                    acc[to] += pieces[m * BS:(m + 1) * BS]
        return carry

    lax.fori_loop(0, GROUP // UNROLL, rows, 0)

    @pl.when(step == MAIN_STEPS - 1)
    def _():
        prev_ref[...] = acc[0:CB].astype(jnp.bfloat16)
        own_ref[...] = acc[CB:2 * CB]
        next_ref[...] = acc[2 * CB:3 * CB].astype(jnp.bfloat16)


def halo_part(codes, touch, targets, p_prev, p_next, part, a_blocks, p_local):
    whole = lambda s, *_: (0, 0, 0)
    rows = (CB, BS, KC * BS)
    return pl.pallas_call(
        halo_kernel,
        grid_spec=pltpu.PrefetchScalarGridSpec(
            num_scalar_prefetch=3,
            grid=(MAIN_STEPS,),
            in_specs=[
                pl.BlockSpec((HALO, BS, KP * BS), whole),
                pl.BlockSpec((HALO, BS, KP * BS), whole),
                pl.BlockSpec((GROUP, BS, KC * BS), lambda s, *_: (s, 0, 0)),
                pl.BlockSpec((GROUP, BS, 2 * BS), lambda s, *_: (s, 0, KA // 2 - 1)),
                pl.BlockSpec((GROUP, BS, KP * BS), lambda s, *_: (s, 0, 0)),
            ],
            out_specs=[pl.BlockSpec(rows, whole)] * 3,
            scratch_shapes=[
                pltpu.VMEM((2 * HALO * SUBSETS, BS, 128), jnp.bfloat16),
                pltpu.VMEM((TARGETS, BS, KC * BS), jnp.float32),
            ],
        ),
        out_shape=[
            jax.ShapeDtypeStruct(rows, jnp.float32),
            jax.ShapeDtypeStruct(rows, jnp.bfloat16),
            jax.ShapeDtypeStruct(rows, jnp.bfloat16),
        ],
        compiler_params=pltpu.CompilerParams(vmem_limit_bytes=54 * 1024 * 1024),
        cost_estimate=pl.CostEstimate(flops=16_000_000_000, bytes_accessed=20_000_000, transcendentals=0),
    )(codes, touch, targets, p_prev, p_next, part, a_blocks, p_local)


def exchange_kernel(n_grp, n_dev, own_hbm, prev_ref, next_ref, out_ref, own_ref, from_prev, from_next, sems_out,
                    sems_in, own_sem):
    own_copy = pltpu.make_async_copy(own_hbm, own_ref, own_sem)
    own_copy.start()
    g = lax.axis_index("grp")
    d = lax.axis_index("dev")
    count = n_grp * n_dev
    position = g * n_dev + d
    after = lax.rem(position + 1, count)
    before = lax.rem(position + count - 1, count)
    after_id = (after // n_dev, lax.rem(after, n_dev))
    before_id = (before // n_dev, lax.rem(before, n_dev))
    up_id = (lax.rem(g + 1, n_grp), d)
    down_id = (lax.rem(g + n_grp - 1, n_grp), d)

    barrier = pltpu.get_barrier_semaphore()
    for other in (after_id, before_id, up_id, down_id):
        pl.semaphore_signal(barrier, inc=1, device_id=other, device_id_type=MESH)
    pl.semaphore_wait(barrier, 4)

    def copy(source, target, kind, r, device):
        return pltpu.make_async_remote_copy(
            src_ref=source, dst_ref=target, send_sem=sems_out.at[kind, r], recv_sem=sems_in.at[kind, r],
            device_id=device, device_id_type=MESH)

    sent = []
    to_after = [copy(next_ref.at[r], from_prev.at[r], 0, r, after_id) for r in range(CB)]
    to_before = [copy(prev_ref.at[r], from_next.at[r], 1, r, before_id) for r in range(CB)]
    for r in range(CB):
        to_after[r].start()
        to_before[r].start()
    own_copy.wait()
    below = lax.rem(g + n_grp - 1, n_grp)
    above = lax.rem(g + 1, n_grp)
    ups, downs, relays = [], [], []

    def relay(r):
        if r < CB // 2:
            ups[r].wait_recv()
            block = below * CB + r
            onward = copy(out_ref.at[block], out_ref.at[block], 4, r, up_id)
        else:
            downs[r].wait_recv()
            block = above * CB + r
            onward = copy(out_ref.at[block], out_ref.at[block], 4, r, down_id)
        onward.start()
        relays.append(onward)

    for r in range(CB):
        to_after[r].wait_recv()
        to_before[r].wait_recv()
        total = own_ref[r] + from_prev[r].astype(jnp.float32) + from_next[r].astype(jnp.float32)
        block = g * CB + r
        out_ref[block] = total.astype(jnp.bfloat16)
        up = copy(out_ref.at[block], out_ref.at[block], 2, r, up_id)
        down = copy(out_ref.at[block], out_ref.at[block], 3, r, down_id)
        up.start()
        down.start()
        ups.append(up)
        downs.append(down)
        if r >= 1:
            relay(r - 1)
    relay(CB - 1)
    for r in range(CB):
        if r < CB // 2:
            downs[r].wait_recv()
        else:
            ups[r].wait_recv()
        relays[r].wait_recv()
        for c in (to_after[r], to_before[r], ups[r], downs[r], relays[r]):
            c.wait_send()


def exchange(own, to_prev, to_next):
    n_grp, n_dev = lax.axis_size("grp"), lax.axis_size("dev")
    rows = (CB, BS, KC * BS)
    return pl.pallas_call(
        functools.partial(exchange_kernel, n_grp, n_dev),
        out_shape=jax.ShapeDtypeStruct((n_grp * CB, BS, KC * BS), jnp.bfloat16),
        in_specs=[pl.BlockSpec(memory_space=pl.ANY)] * 3,
        out_specs=pl.BlockSpec(memory_space=pltpu.VMEM),
        scratch_shapes=[
            pltpu.VMEM(rows, jnp.float32),
            pltpu.VMEM(rows, jnp.bfloat16),
            pltpu.VMEM(rows, jnp.bfloat16),
            pltpu.SemaphoreType.DMA((5, CB)),
            pltpu.SemaphoreType.DMA((5, CB)),
            pltpu.SemaphoreType.DMA,
        ],
        compiler_params=pltpu.CompilerParams(collective_id=0, has_side_effects=True,
                                             vmem_limit_bytes=32 * 1024 * 1024),
    )(own, to_prev, to_next)


def on_device(a_blocks, a_cols, p_blocks, ap_slots, p_touch, owner_dev, owner_row):
    axes = ("grp", "dev")
    position = lax.axis_index(axes)
    count = lax.axis_size(axes)
    up = [(i, (i + 1) % count) for i in range(count)]
    down = [(j, i) for i, j in up]
    p_prev = lax.ppermute(p_blocks[FB - HALO:], axes, up)
    p_next = lax.ppermute(p_blocks[:HALO], axes, down)

    local = a_cols - position * FB
    slots = ap_slots.reshape(FB, KA, KP)
    weights = jnp.int32(1) << jnp.arange(KP, dtype=jnp.int32)
    hits = slots[:, :, :, None] == jnp.arange(KC, dtype=jnp.int32)
    subset = jnp.sum(jnp.where(hits, weights[:, None], 0), axis=2)
    inside = (local >= 0) & (local < FB)
    here = jnp.where((subset == 0) | ~inside[:, :, None], 0, local[:, :, None] * SUBSETS + subset)
    nearby = jnp.where(local < 0, local + HALO, local - FB + HALO)[:, KA - 2:, None]
    there = jnp.where((subset[:, KA - 2:] == 0) | inside[:, KA - 2:, None], 0, nearby * SUBSETS + subset[:, KA - 2:])
    edge = ((position == 0) | (position == count - 1)).astype(jnp.int32).reshape(1)
    targets = (owner_dev[:, 0] - position + 1) * CB + owner_row
    part = local_part(here.reshape(-1), edge, p_blocks, a_blocks)
    own, to_prev, to_next = halo_part(there.reshape(-1), p_touch.reshape(-1), targets, p_prev, p_next, part,
                                      a_blocks, p_blocks)
    return exchange(own, to_prev, to_next)


def solution(mesh):
    placed = (
        P(("grp", "dev"), None, None),
        P(("grp", "dev"), None),
        P(("grp", "dev"), None, None),
        P(("grp", "dev"), None),
        P(("grp", "dev"), None),
        P(("grp", "dev"), None),
        P(("grp", "dev")),
    )
    return jax.shard_map(
        on_device, mesh=mesh, in_specs=placed, out_specs=P("dev", None, None), check_vma=False
    )
```

time: 137 us -> 115 us (0.84); the launches traced: 135 us -> 115 us
  waiting for transfers between devices: 17.2 us -> 0.01 us
  Pallas kernels: 101 us -> 95.1 us
  local copies, waits for them, and re-layouts: 8.25 us -> 10.8 us
    pallas_call x1 -> x2, Pallas kernels: 68.1 us -> 57.6 us  [the longest x1 30.9 us: local_part(): pl.pallas_call(local_kernel, grid_spec=pltpu.PrefetchScalarGridSpec(num_s...]
    ppermute x1, waiting for transfers between devices: 9.74 us -> 0.01 us  [on_device(): p_next = lax.ppermute(p_blocks[:HALO], axes, down)]
    ppermute x1, waiting for transfers between devices: 7.44 us -> 0.01 us  [on_device(): p_prev = lax.ppermute(p_blocks[FB - HALO:], axes, up)]
    pallas_call x1, Pallas kernels: 32.6 us -> 37.4 us  [exchange(): pl.pallas_call(functools.partial(exchange_kernel, n_grp, n_dev), out_shap...]
    unnamed x18 -> x20, local copies, waits for them, and re-layouts: 4.76 us -> 6.95 us
  transfers between devices with their start and end apart: 2 -> 2, of which waited for: 2 -> 0; matrix products, arithmetic and copies ran while one was open for 2% -> 3% of each run, Pallas kernels for 0% -> 27%
where the time goes in v2:
time: 115 us
  Pallas kernels  95.1 us (83%)
  local copies, waits for them, and re-layouts  10.8 us (9%)
  starting transfers between devices  8.28 us (7%)
    pallas_call x1, Pallas kernels, exchange(): pl.pallas_call(functools.partial(exchange_kernel, n_grp, n_dev), out_shap...  37.4 us
    pallas_call x1, Pallas kernels, local_part(): pl.pallas_call(local_kernel, grid_spec=pltpu.PrefetchScalarGridSpec(num_s...  30.9 us
    pallas_call x1, Pallas kernels, halo_part(): pl.pallas_call(halo_kernel, grid_spec=pltpu.PrefetchScalarGridSpec(num_sc...  26.7 us
    ppermute x1, starting transfers between devices, on_device(): p_next = lax.ppermute(p_blocks[:HALO], axes, down)  8.27 us
    unnamed x20, local copies, waits for them, and re-layouts  6.95 us
  transfers between devices with their start and end apart: 2, of which 0 were waited for; matrix products, arithmetic and copies ran while one was open for 3% of the time, Pallas kernels for 27%

profile of v2, /device:TPU:0, one launch (start us, length us, event | category | flops | bytes accessed | tf_op | source)
XLA Modules:
  0.0 115.0 jit_solution(6464437846545163365)
XLA Ops:
  0.0 0.0 copy-start.5
  0.0 0.0 copy-start.8
  0.0 0.0 copy-start.6
  0.0 0.0 copy-start.4
  0.0 0.0 copy-start.7
  0.0 1.7 %fusion.1 = (bf16[32,64,256]{2,1,0:T(8,128)(2,1)S(1)}, bf16[32,64,256]{2,1,0:T(8,128)(2,1)S(1)}) fusion(bf16[128,64,256]{2,1,0:T(8,128)(2,1)} %p_ref.3), kind=kLoop, calls=%fused_computation.11 | loop fusion | bytes 4194304 | tf_op jit(solution)/shard_map/slice | solution.py:302
  1.8 8.3 %collective-permute-start.1 = (bf16[32,64,256]{2,1,0:T(8,128)(2,1)S(1)}, bf16[32,64,256]{2,1,0:T(8,128)(2,1)}, u32[]{:S(2)}, u32[]{:S(2)}) collective-permute-start(bf16[32,64,256]{2,1,0:T(8,128)(2,1)S(1)} %get-tuple-element.13), channel_id=1, source_target_pairs={{1,0},{2,1},{3,2},{4,3},{5,4},{6,5},{7,6},{8,7},{9,8},{10,9},{11,1... | collective-permute-start | bytes 3145736 | tf_op jit(solution)/shard_map/ppermute | solution.py:302
  10.0 0.0 collective-permute-start
  10.0 0.0 copy-done.5
  10.1 0.0 copy-done.8
  10.1 0.0 copy-done.6
  10.1 0.1 copy.20
  10.3 0.7 reshape.36.touch
  10.9 0.0 copy-done.4
  10.9 0.1 select_reduce_fusion
  11.0 0.1 copy.19
  11.2 0.8 reshape.35.codes
  12.0 0.2 copy.21
  12.2 0.3 select_n.24.codes
  12.5 0.0 copy-done.7
  12.5 0.6 add.50.targets
  13.1 0.0 copy-start
  13.1 2.2 %copy-done = bf16[128,64,256]{2,1,0:T(8,128)(2,1)S(1)} copy-done((bf16[128,64,256]{2,1,0:T(8,128)(2,1)S(1)}, bf16[128,64,256]{2,1,0:T(8,128)(2,1)}, u32[]{:S(2)}) %copy-start) | copy-done | bytes 4194328
  15.3 30.9 %shard_map.73.part_ref = bf16[128,64,512]{2,1,0:T(8,128)(2,1)} custom-call(s32[8192]{0:T(1024)S(1)} %select_n.24.codes, s32[1]{0:T(128)} %bitcast.2.edge, bf16[128,64,256]{2,1,0:T(8,128)(2,1)S(1)} %copy-done, bf16[128,64,512]{2,1,0:T(8,128)(2,1)} %a_ref.3), custom_call_target="tpu_custom_call" | custom-call | flops 16000000000 | bytes 20000000 | tf_op jit(solution)/shard_map/pallas_call | solution.py:108
  46.2 0.0 collective-permute-done.1.p_next
  46.2 0.0 collective-permute-done.p_prev
  46.2 26.7 %shard_map.74 = (f32[8,64,512]{2,1,0:T(8,128)}, bf16[8,64,512]{2,1,0:T(8,128)(2,1)}, bf16[8,64,512]{2,1,0:T(8,128)(2,1)}) custom-call(s32[2048]{0:T(1024)} %reshape.35.codes, s32[512]{0:T(512)} %reshape.36.touch, s32[224]{0:T(256)} %add.50.targets, bf16[32,64,256]{2,1,0:T(8,128)(2,1)} %collective-permute-done.p_prev, ...), custom_call_target="tpu_custom_call" | custom-call | flops 16000000000 | bytes 20000000 | tf_op jit(solution)/shard_map/pallas_call | solution.py:173
  72.9 1.2 %copy-done.1 = f32[8,64,512]{2,1,0:T(8,128)S(1)} copy-done((f32[8,64,512]{2,1,0:T(8,128)S(1)}, f32[8,64,512]{2,1,0:T(8,128)}, u32[]{:S(2)}) %copy-start.1) | copy-done | bytes 1048600
  74.1 1.0 copy-done.2
  75.2 1.0 copy-done.3
  76.2 37.4 %shard_map.75 = bf16[32,64,512]{2,1,0:T(8,128)(2,1)S(1)} custom-call(f32[8,64,512]{2,1,0:T(8,128)S(1)} %copy-done.1, bf16[8,64,512]{2,1,0:T(8,128)(2,1)S(1)} %copy-done.2, bf16[8,64,512]{2,1,0:T(8,128)(2,1)S(1)} %copy-done.3), custom_call_target="tpu_custom_call" | custom-call | tf_op jit(solution)/shard_map/pallas_call | solution.py:277
  113.7 1.3 %copy.23 = bf16[32,64,512]{2,1,0:T(8,128)(2,1)} copy(bf16[32,64,512]{2,1,0:T(8,128)(2,1)S(1)} %shard_map.75) | data formatting | bytes 4194304
  (11 shorter events, 0.1 us)
Async XLA Ops:
  0.0 10.0 %copy-start.5 = (s32[128,8]{0,1:T(8,128)S(1)}, s32[128,8]{0,1:T(8,128)}, u32[]{:S(2)}) copy-start(s32[128,8]{0,1:T(8,128)} %param.8) | copy-start | bytes 12292
  0.0 10.1 %copy-start.8 = (s32[224,1]{0,1:T(1,128)S(1)}, s32[224,1]{0,1:T(1,128)}, u32[]{:S(2)}) copy-start(s32[224,1]{0,1:T(1,128)} %param.12) | copy-start | bytes 2692
  0.0 10.1 %copy-start.6 = (s32[128,4]{0,1:T(4,128)S(1)}, s32[128,4]{0,1:T(4,128)}, u32[]{:S(2)}) copy-start(s32[128,4]{0,1:T(4,128)} %param.11) | copy-start | bytes 6148
  0.0 10.9 %copy-start.4 = (s32[128,32]{0,1:T(8,128)S(1)}, s32[128,32]{0,1:T(8,128)}, u32[]{:S(2)}) copy-start(s32[128,32]{0,1:T(8,128)} %param.10) | copy-start | bytes 49156
  0.0 12.5 %copy-start.7 = (s32[224]{0:T(256)S(1)}, s32[224]{0:T(256)}, u32[]{:S(2)}) copy-start(s32[224]{0:T(256)} %param.13) | copy-start | bytes 2692
  1.8 44.4 %collective-permute-start.1 = (bf16[32,64,256]{2,1,0:T(8,128)(2,1)S(1)}, bf16[32,64,256]{2,1,0:T(8,128)(2,1)}, u32[]{:S(2)}, u32[]{:S(2)}) collective-permute-start(bf16[32,64,256]{2,1,0:T(8,128)(2,1)S(1)} %get-tuple-element.13), channel_id=1, source_target_pairs={{1,0},{2,1},{3,2},{4,3},{5,4},{6,5},{7,6},{8,7},{9,8},{10,9},{11,1... | collective-permute-start | bytes 3145736 | tf_op jit(solution)/shard_map/ppermute | solution.py:302
  10.0 36.2 %collective-permute-start = (bf16[32,64,256]{2,1,0:T(8,128)(2,1)S(1)}, bf16[32,64,256]{2,1,0:T(8,128)(2,1)}, u32[]{:S(2)}, u32[]{:S(2)}) collective-permute-start(bf16[32,64,256]{2,1,0:T(8,128)(2,1)S(1)} %get-tuple-element.14), channel_id=1, source_target_pairs={{0,1},{1,2},{2,3},{3,4},{4,5},{5,6},{6,7},{7,8},{8,9},{9,10},{10,1... | collective-permute-start | bytes 3145736 | tf_op jit(solution)/shard_map/ppermute | solution.py:301
  13.1 2.2 %copy-start = (bf16[128,64,256]{2,1,0:T(8,128)(2,1)S(1)}, bf16[128,64,256]{2,1,0:T(8,128)(2,1)}, u32[]{:S(2)}) copy-start(bf16[128,64,256]{2,1,0:T(8,128)(2,1)} %p_ref.3) | copy-start | bytes 12582916
  72.9 1.2 %copy-start.1 = (f32[8,64,512]{2,1,0:T(8,128)S(1)}, f32[8,64,512]{2,1,0:T(8,128)}, u32[]{:S(2)}) copy-start(f32[8,64,512]{2,1,0:T(8,128)} %get-tuple-element.8.own_hbm) | copy-start | bytes 3145732
  74.1 1.0 copy-start.2
  75.2 1.0 copy-start.3

commit v3 on v2

--- a/solution.py
+++ b/solution.py
@@ -58,8 +58,8 @@
     for k in range(blocks):
         tiles = []
         for s in range(4 * nt, 4 * nt + 4, 2):
-            at = first + k * KC + s
-            tiles.append(jnp.where(left, table[codes[at]], table[codes[at + 1]]))
+            at = (k * KC + s) * FB + first
+            tiles.append(jnp.where(left, table[codes[at]], table[codes[at + FB]]))
         rows.append(jnp.concatenate(tiles, axis=1))
     return jnp.concatenate(rows, axis=0)
 
@@ -85,7 +85,7 @@
                 for nt in range(2):
                     total = None
                     for low, high in cuts:
-                        weights = coefficients(table, codes, (first + r) * (KA * KC) + low * KC, high - low, nt, left)
+                        weights = coefficients(table, codes, low * KC * FB + first + r, high - low, nt, left)
                         part = jnp.dot(a_ref[r, :, low * BS:high * BS], weights,
                                        preferred_element_type=jnp.float32)
                         total = part if total is None else total + part
@@ -118,7 +118,7 @@
             scratch_shapes=[pltpu.VMEM((FB * SUBSETS, BS, 128), jnp.bfloat16)],
         ),
         out_shape=jax.ShapeDtypeStruct((FB, BS, KC * BS), jnp.bfloat16),
-        compiler_params=pltpu.CompilerParams(vmem_limit_bytes=44 * 1024 * 1024),
+        compiler_params=pltpu.CompilerParams(vmem_limit_bytes=58 * 1024 * 1024),
         cost_estimate=pl.CostEstimate(flops=16_000_000_000, bytes_accessed=20_000_000, transcendentals=0),
     )(codes, edge, p_local, a_blocks)
 
@@ -143,7 +143,7 @@
                 i = step * GROUP + r
                 halves = []
                 for nt in range(2):
-                    weights = coefficients(table, codes, i * (2 * KC), 2, nt, left)
+                    weights = coefficients(table, codes, i, 2, nt, left)
                     total = jnp.dot(a_ref[r], weights, preferred_element_type=jnp.float32)
                     total = total + part_ref[r, :, nt * 256:(nt + 1) * 256].astype(jnp.float32)
                     halves.append(total.astype(jnp.bfloat16))
@@ -154,7 +154,7 @@
                 pieces = lax.dot_general(p_ref[r], kept[u - 1], (((0,), (0,)), ((), ())),
                                          preferred_element_type=jnp.float32)
                 for m in range(KP):
-                    to = targets[touch[i * KP + m]]
+                    to = targets[touch[m * FB + i]]
                     acc[to] += pieces[m * BS:(m + 1) * BS]
         return carry
 
@@ -193,7 +193,7 @@
             jax.ShapeDtypeStruct(rows, jnp.bfloat16),
             jax.ShapeDtypeStruct(rows, jnp.bfloat16),
         ],
-        compiler_params=pltpu.CompilerParams(vmem_limit_bytes=54 * 1024 * 1024),
+        compiler_params=pltpu.CompilerParams(vmem_limit_bytes=49 * 1024 * 1024),
         cost_estimate=pl.CostEstimate(flops=16_000_000_000, bytes_accessed=20_000_000, transcendentals=0),
     )(codes, touch, targets, p_prev, p_next, part, a_blocks, p_local)
 
@@ -226,13 +226,13 @@
     sent = []
     to_after = [copy(next_ref.at[r], from_prev.at[r], 0, r, after_id) for r in range(CB)]
     to_before = [copy(prev_ref.at[r], from_next.at[r], 1, r, before_id) for r in range(CB)]
-    for r in range(CB):
+    for r in range(3):
         to_after[r].start()
         to_before[r].start()
     own_copy.wait()
     below = lax.rem(g + n_grp - 1, n_grp)
     above = lax.rem(g + 1, n_grp)
-    ups, downs, relays = [], [], []
+    ups, downs, relays = [], [], [None] * CB
 
     def relay(r):
         if r < CB // 2:
@@ -244,11 +244,16 @@
             block = above * CB + r
             onward = copy(out_ref.at[block], out_ref.at[block], 4, r, down_id)
         onward.start()
-        relays.append(onward)
+        relays[r] = onward
 
     for r in range(CB):
         to_after[r].wait_recv()
         to_before[r].wait_recv()
+        if r + 3 < CB:
+            to_after[r].wait_send()
+            to_before[r].wait_send()
+            to_after[r + 3].start()
+            to_before[r + 3].start()
         total = own_ref[r] + from_prev[r].astype(jnp.float32) + from_next[r].astype(jnp.float32)
         block = g * CB + r
         out_ref[block] = total.astype(jnp.bfloat16)
@@ -258,17 +263,19 @@
         down.start()
         ups.append(up)
         downs.append(down)
-        if r >= 1:
-            relay(r - 1)
-    relay(CB - 1)
+    for r in range(CB):
+        relay(r // 2 + (r % 2) * (CB // 2))
     for r in range(CB):
         if r < CB // 2:
             downs[r].wait_recv()
         else:
             ups[r].wait_recv()
         relays[r].wait_recv()
-        for c in (to_after[r], to_before[r], ups[r], downs[r], relays[r]):
+        for c in (ups[r], downs[r], relays[r]):
             c.wait_send()
+        if r + 3 >= CB:
+            to_after[r].wait_send()
+            to_before[r].wait_send()
 
 
 def exchange(own, to_prev, to_next):
@@ -296,24 +303,25 @@
     axes = ("grp", "dev")
     position = lax.axis_index(axes)
     count = lax.axis_size(axes)
-    up = [(i, (i + 1) % count) for i in range(count)]
+    up = [(i, i + 1) for i in range(count - 1)]
     down = [(j, i) for i, j in up]
     p_prev = lax.ppermute(p_blocks[FB - HALO:], axes, up)
     p_next = lax.ppermute(p_blocks[:HALO], axes, down)
 
-    local = a_cols - position * FB
-    slots = ap_slots.reshape(FB, KA, KP)
+    local = a_cols.T - position * FB
+    slots = ap_slots.T.reshape(KA, KP, FB)
     weights = jnp.int32(1) << jnp.arange(KP, dtype=jnp.int32)
-    hits = slots[:, :, :, None] == jnp.arange(KC, dtype=jnp.int32)
-    subset = jnp.sum(jnp.where(hits, weights[:, None], 0), axis=2)
+    hits = slots[:, :, None, :] == jnp.arange(KC, dtype=jnp.int32)[:, None]
+    subset = jnp.sum(jnp.where(hits, weights[:, None, None], 0), axis=1)
     inside = (local >= 0) & (local < FB)
-    here = jnp.where((subset == 0) | ~inside[:, :, None], 0, local[:, :, None] * SUBSETS + subset)
-    nearby = jnp.where(local < 0, local + HALO, local - FB + HALO)[:, KA - 2:, None]
-    there = jnp.where((subset[:, KA - 2:] == 0) | inside[:, KA - 2:, None], 0, nearby * SUBSETS + subset[:, KA - 2:])
+    here = jnp.where((subset == 0) | ~inside[:, None, :], 0, local[:, None, :] * SUBSETS + subset)
+    nearby = jnp.where(local < 0, local + HALO, local - FB + HALO)[KA - 2:, None, :]
+    subset, inside = subset[KA - 2:], inside[KA - 2:, None, :]
+    there = jnp.where((subset == 0) | inside, 0, nearby * SUBSETS + subset)
     edge = ((position == 0) | (position == count - 1)).astype(jnp.int32).reshape(1)
     targets = (owner_dev[:, 0] - position + 1) * CB + owner_row
     part = local_part(here.reshape(-1), edge, p_blocks, a_blocks)
-    own, to_prev, to_next = halo_part(there.reshape(-1), p_touch.reshape(-1), targets, p_prev, p_next, part,
+    own, to_prev, to_next = halo_part(there.reshape(-1), p_touch.T.reshape(-1), targets, p_prev, p_next, part,
                                       a_blocks, p_blocks)
     return exchange(own, to_prev, to_next)
 

time: 115 us -> 100 us (0.87)
  local copies, waits for them, and re-layouts: 10.8 us -> 4.1 us
  Pallas kernels: 95.1 us -> 90.8 us
  starting transfers between devices: 8.28 us -> 4.38 us
    ppermute x1, starting transfers between devices: 8.27 us -> 1.28 us  [on_device(): p_next = lax.ppermute(p_blocks[:HALO], axes, down)]
    unnamed x20 -> x11, local copies, waits for them, and re-layouts: 6.95 us -> 1.34 us
    ppermute x1, starting transfers between devices: 0.01 us -> 3.1 us  [on_device(): p_prev = lax.ppermute(p_blocks[FB - HALO:], axes, up)]
    pallas_call x1, Pallas kernels: 37.4 us -> 34.5 us  [exchange(): pl.pallas_call(functools.partial(exchange_kernel, n_grp, n_dev), out_shap...]
    pallas_call x1, Pallas kernels: 26.7 us -> 24.7 us  [halo_part(): pl.pallas_call(halo_kernel, grid_spec=pltpu.PrefetchScalarGridSpec(num_sc...]
    reshape x2 -> x0, local copies, waits for them, and re-layouts: 1.49 us -> none  [the longest x1 0.79 us: on_device(): there.reshape(-1)]
  transfers between devices with their start and end apart: 2 -> 2, of which waited for: 0 -> 0; matrix products, arithmetic and copies ran while one was open for 3% -> 1% of each run, Pallas kernels for 27% -> 32%
where the time goes in v3:
time: 100 us
  Pallas kernels  90.8 us (91%)
  starting transfers between devices  4.38 us (4%)
  local copies, waits for them, and re-layouts  4.1 us (4%)
    pallas_call x1, Pallas kernels, exchange(): pl.pallas_call(functools.partial(exchange_kernel, n_grp, n_dev), out_shap...  34.5 us
    pallas_call x1, Pallas kernels, local_part(): pl.pallas_call(local_kernel, grid_spec=pltpu.PrefetchScalarGridSpec(num_s...  31.6 us
    pallas_call x1, Pallas kernels, halo_part(): pl.pallas_call(halo_kernel, grid_spec=pltpu.PrefetchScalarGridSpec(num_sc...  24.7 us
    ppermute x1, starting transfers between devices, on_device(): p_prev = lax.ppermute(p_blocks[FB - HALO:], axes, up)  3.1 us
    slice x1, local copies, waits for them, and re-layouts, on_device(): p_next = lax.ppermute(p_blocks[:HALO], axes, down)  2.76 us
  transfers between devices with their start and end apart: 2, of which 0 were waited for; matrix products, arithmetic and copies ran while one was open for 1% of the time, Pallas kernels for 32%

profile of v3, /device:TPU:0, one launch (start us, length us, event | category | flops | bytes accessed | tf_op | source)
XLA Modules:
  0.0 100.1 jit_solution(2561371586423662574)
XLA Ops:
  0.0 0.0 copy-start.2
  0.0 0.0 copy-start.4
  0.0 0.0 copy-start.3
  0.0 0.0 copy-start.1
  0.0 2.8 %fusion.1 = (bf16[32,64,256]{2,1,0:T(8,128)(2,1)}, bf16[32,64,256]{2,1,0:T(8,128)(2,1)S(1)}) fusion(bf16[128,64,256]{2,1,0:T(8,128)(2,1)} %p_ref.3), kind=kLoop, calls=%fused_computation.11 | loop fusion | bytes 4194304 | tf_op jit(solution)/shard_map/slice | solution.py:309
  2.8 1.3 %collective-permute-start.1 = (bf16[32,64,256]{2,1,0:T(8,128)(2,1)}, bf16[32,64,256]{2,1,0:T(8,128)(2,1)S(1)}, u32[]{:S(2)}, u32[]{:S(2)}) collective-permute-start(bf16[32,64,256]{2,1,0:T(8,128)(2,1)} %get-tuple-element.13), channel_id=1, source_target_pairs={{1,0},{2,1},{3,2},{4,3},{5,4},{6,5},{7,6},{8,7},{9,8},{10,9},{11,1... | collective-permute-start | bytes 3145736 | tf_op jit(solution)/shard_map/ppermute | solution.py:309
  4.1 3.1 %collective-permute-start = (bf16[32,64,256]{2,1,0:T(8,128)(2,1)S(1)}, bf16[32,64,256]{2,1,0:T(8,128)(2,1)S(1)}, u32[]{:S(2)}, u32[]{:S(2)}) collective-permute-start(bf16[32,64,256]{2,1,0:T(8,128)(2,1)S(1)} %get-tuple-element.14), channel_id=1, source_target_pairs={{0,1},{1,2},{2,3},{3,4},{4,5},{5,6},{6,7},{7,8},{8,9},{9,10},{10,1... | collective-permute-start | bytes 3145736 | tf_op jit(solution)/shard_map/ppermute | solution.py:308
  7.2 0.0 copy-done.2
  7.2 0.0 copy-done.4
  7.3 0.0 copy-done.3
  7.3 0.0 copy-done.1
  7.3 0.1 select_reduce_fusion
  7.4 0.6 select_bitcast_fusion.codes
  8.0 0.0 copy-start
  8.0 31.6 %shard_map.73.part_ref = bf16[128,64,512]{2,1,0:T(8,128)(2,1)} custom-call(s32[8192]{0:T(1024)} %select_bitcast_fusion.codes, s32[1]{0:T(128)} %bitcast.10.edge, bf16[128,64,256]{2,1,0:T(8,128)(2,1)} %p_ref.3, bf16[128,64,512]{2,1,0:T(8,128)(2,1)} %a_ref.3), custom_call_target="tpu_custom_call" | custom-call | flops 16000000000 | bytes 20000000 | tf_op jit(solution)/shard_map/pallas_call | solution.py:108
  39.6 0.0 collective-permute-done.1.p_next
  39.6 0.0 collective-permute-done.p_prev
  39.6 0.0 copy-done
  39.6 24.7 %shard_map.74 = (f32[8,64,512]{2,1,0:T(8,128)S(1)}, bf16[8,64,512]{2,1,0:T(8,128)(2,1)S(1)}, bf16[8,64,512]{2,1,0:T(8,128)(2,1)S(1)}) custom-call(s32[2048]{0:T(1024)S(1)} %select_bitcast_fusion.1.codes, s32[512]{0:T(512)S(1)} %bitcast.19, s32[224]{0:T(256)S(1)} %add.52.targets, bf16[32,64,256]{2,1,0:T(8,128)(2,1)S(1)} %collective-permute-done.p_prev, ...), custom_call_target="tpu_custom_call" | custom-call | flops 16000000000 | bytes 20000000 | tf_op jit(solution)/shard_map/pallas_call | solution.py:173
  64.3 34.5 %shard_map.75 = bf16[32,64,512]{2,1,0:T(8,128)(2,1)S(1)} custom-call(f32[8,64,512]{2,1,0:T(8,128)S(1)} %get-tuple-element.8.own_hbm, bf16[8,64,512]{2,1,0:T(8,128)(2,1)S(1)} %get-tuple-element.9.prev_ref, bf16[8,64,512]{2,1,0:T(8,128)(2,1)S(1)} %get-tuple-element.10.next_ref), custom_call_target="tpu_custom_call" | custom-call | tf_op jit(solution)/shard_map/pallas_call | solution.py:284
  98.8 1.3 %copy.9 = bf16[32,64,512]{2,1,0:T(8,128)(2,1)} copy(bf16[32,64,512]{2,1,0:T(8,128)(2,1)S(1)} %shard_map.75) | data formatting | bytes 4194304
  (8 shorter events, 0.1 us)
Async XLA Ops:
  0.0 7.2 %copy-start.2 = (s32[128,8]{0,1:T(8,128)S(1)}, s32[128,8]{0,1:T(8,128)}, u32[]{:S(2)}) copy-start(s32[128,8]{0,1:T(8,128)} %param.8) | copy-start | bytes 12292
  0.0 7.2 %copy-start.4 = (s32[224,1]{0,1:T(1,128)S(1)}, s32[224,1]{0,1:T(1,128)}, u32[]{:S(2)}) copy-start(s32[224,1]{0,1:T(1,128)} %param.12) | copy-start | bytes 2692
  0.0 7.3 %copy-start.3 = (s32[224]{0:T(256)S(1)}, s32[224]{0:T(256)}, u32[]{:S(2)}) copy-start(s32[224]{0:T(256)} %param.13) | copy-start | bytes 2692
  0.0 7.3 %copy-start.1 = (s32[128,32]{0,1:T(8,128)S(1)}, s32[128,32]{0,1:T(8,128)}, u32[]{:S(2)}) copy-start(s32[128,32]{0,1:T(8,128)} %param.10) | copy-start | bytes 49156
  2.8 36.8 %collective-permute-start.1 = (bf16[32,64,256]{2,1,0:T(8,128)(2,1)}, bf16[32,64,256]{2,1,0:T(8,128)(2,1)S(1)}, u32[]{:S(2)}, u32[]{:S(2)}) collective-permute-start(bf16[32,64,256]{2,1,0:T(8,128)(2,1)} %get-tuple-element.13), channel_id=1, source_target_pairs={{1,0},{2,1},{3,2},{4,3},{5,4},{6,5},{7,6},{8,7},{9,8},{10,9},{11,1... | collective-permute-start | bytes 3145736 | tf_op jit(solution)/shard_map/ppermute | solution.py:309
  4.1 35.5 %collective-permute-start = (bf16[32,64,256]{2,1,0:T(8,128)(2,1)S(1)}, bf16[32,64,256]{2,1,0:T(8,128)(2,1)S(1)}, u32[]{:S(2)}, u32[]{:S(2)}) collective-permute-start(bf16[32,64,256]{2,1,0:T(8,128)(2,1)S(1)} %get-tuple-element.14), channel_id=1, source_target_pairs={{0,1},{1,2},{2,3},{3,4},{4,5},{5,6},{6,7},{7,8},{8,9},{9,10},{10,1... | collective-permute-start | bytes 3145736 | tf_op jit(solution)/shard_map/ppermute | solution.py:308
  8.0 31.6 %copy-start = (s32[128,4]{0,1:T(4,128)S(1)}, s32[128,4]{0,1:T(4,128)}, u32[]{:S(2)}) copy-start(s32[128,4]{0,1:T(4,128)} %param.11) | copy-start | bytes 6148

commit v4 on v3

--- a/solution.py
+++ b/solution.py
@@ -20,6 +20,7 @@
 LOCAL_STEPS = FB // P_ROWS
 GROUP = 16
 UNROLL = 8
+SEND_STEP = 2
 MAIN_STEPS = FB // GROUP
 TARGETS = 3 * CB
 MESH = pl.DeviceIdType.MESH
@@ -64,9 +65,51 @@
     return jnp.concatenate(rows, axis=0)
 
 
-def local_kernel(codes, edge, p_ref, a_ref, out_ref, table):
+def local_kernel(n_grp, n_dev, codes, p_hbm, p_ref, a_ref, out_ref, prev_out, next_out, table, sems_out,
+                 sems_in):
     step = pl.program_id(0)
     left = left_half()
+    count = n_grp * n_dev
+    position = lax.axis_index("grp") * n_dev + lax.axis_index("dev")
+    has_before = position > 0
+    has_after = position < count - 1
+    after = jnp.minimum(position + 1, count - 1)
+    before = jnp.maximum(position - 1, 0)
+    after_id = (after // n_dev, lax.rem(after, n_dev))
+    before_id = (before // n_dev, lax.rem(before, n_dev))
+    barrier = pltpu.get_barrier_semaphore()
+
+    def copy(first, target, kind, device):
+        return pltpu.make_async_remote_copy(
+            src_ref=p_hbm.at[pl.ds(first, HALO)], dst_ref=target, send_sem=sems_out.at[kind],
+            recv_sem=sems_in.at[kind], device_id=device, device_id_type=MESH)
+
+    to_after = copy(FB - HALO, prev_out, 0, after_id)
+    to_before = copy(0, next_out, 1, before_id)
+
+    @pl.when((step == 0) & has_before)
+    def _():
+        pl.semaphore_signal(barrier, inc=1, device_id=before_id, device_id_type=MESH)
+
+    @pl.when((step == 0) & has_after)
+    def _():
+        pl.semaphore_signal(barrier, inc=1, device_id=after_id, device_id_type=MESH)
+
+    @pl.when((step == SEND_STEP) & has_before & has_after)
+    def _():
+        pl.semaphore_wait(barrier, 2)
+        to_after.start()
+        to_before.start()
+
+    @pl.when((step == SEND_STEP) & ~has_before)
+    def _():
+        pl.semaphore_wait(barrier, 1)
+        to_after.start()
+
+    @pl.when((step == SEND_STEP) & ~has_after)
+    def _():
+        pl.semaphore_wait(barrier, 1)
+        to_before.start()
 
     @pl.when(step == 0)
     def _():
@@ -94,36 +137,63 @@
 
         lax.fori_loop(0, GROUP // UNROLL, rows, 0)
 
-    @pl.when((step >= LOCAL_STEPS) & (edge[0] == 0))
+    @pl.when((step >= LOCAL_STEPS) & has_before & has_after)
     def _():
         assemble(((0, 4), (4, KA - 2)))
 
-    @pl.when((step >= LOCAL_STEPS) & (edge[0] != 0))
+    @pl.when((step >= LOCAL_STEPS) & ~has_before)
+    def _():
+        assemble(((0, 4), (4, KA - 1)))
+
+    @pl.when((step >= LOCAL_STEPS) & ~has_after)
     def _():
         assemble(((0, 4), (4, KA)))
 
-
-def local_part(codes, edge, p_local, a_blocks):
+    last = LOCAL_STEPS + MAIN_STEPS - 1
+
+    @pl.when((step == last) & has_before)
+    def _():
+        to_after.wait_recv()
+        to_before.wait_send()
+
+    @pl.when((step == last) & has_after)
+    def _():
+        to_before.wait_recv()
+        to_after.wait_send()
+
+
+def local_part(codes, p_local, a_blocks):
+    n_grp, n_dev = lax.axis_size("grp"), lax.axis_size("dev")
+    halo = jax.ShapeDtypeStruct((HALO, BS, KP * BS), jnp.bfloat16)
     main = lambda s, *_: (jnp.maximum(s - LOCAL_STEPS, 0), 0, 0)
     return pl.pallas_call(
-        local_kernel,
+        functools.partial(local_kernel, n_grp, n_dev),
         grid_spec=pltpu.PrefetchScalarGridSpec(
-            num_scalar_prefetch=2,
+            num_scalar_prefetch=1,
             grid=(LOCAL_STEPS + MAIN_STEPS,),
             in_specs=[
+                pl.BlockSpec(memory_space=pl.ANY),
                 pl.BlockSpec((P_ROWS, BS, KP * BS), lambda s, *_: (jnp.minimum(s, LOCAL_STEPS - 1), 0, 0)),
                 pl.BlockSpec((GROUP, BS, KA * BS), main),
             ],
-            out_specs=pl.BlockSpec((GROUP, BS, KC * BS), main),
-            scratch_shapes=[pltpu.VMEM((FB * SUBSETS, BS, 128), jnp.bfloat16)],
+            out_specs=[
+                pl.BlockSpec((GROUP, BS, KC * BS), main),
+                pl.BlockSpec(memory_space=pl.ANY),
+                pl.BlockSpec(memory_space=pl.ANY),
+            ],
+            scratch_shapes=[
+                pltpu.VMEM((FB * SUBSETS, BS, 128), jnp.bfloat16),
+                pltpu.SemaphoreType.DMA((2,)),
+                pltpu.SemaphoreType.DMA((2,)),
+            ],
         ),
-        out_shape=jax.ShapeDtypeStruct((FB, BS, KC * BS), jnp.bfloat16),
-        compiler_params=pltpu.CompilerParams(vmem_limit_bytes=58 * 1024 * 1024),
+        out_shape=[jax.ShapeDtypeStruct((FB, BS, KC * BS), jnp.bfloat16), halo, halo],
+        compiler_params=pltpu.CompilerParams(collective_id=1, has_side_effects=True, vmem_limit_bytes=58 * 1024 * 1024),
         cost_estimate=pl.CostEstimate(flops=16_000_000_000, bytes_accessed=20_000_000, transcendentals=0),
-    )(codes, edge, p_local, a_blocks)
-
-
-def halo_kernel(codes, touch, targets, p_prev, p_next, part_ref, a_ref, p_ref, own_ref, prev_ref, next_ref,
+    )(codes, p_local, p_local, a_blocks)
+
+
+def halo_kernel(codes, touch, targets, edge, p_prev, p_next, part_ref, a_ref, p_ref, own_ref, prev_ref, next_ref,
                 table, acc):
     step = pl.program_id(0)
     left = left_half()
@@ -131,11 +201,11 @@
     @pl.when(step == 0)
     def _():
         acc[...] = jnp.zeros_like(acc)
-        build_rows(p_prev, 0, table, left)
-        build_rows(p_next, HALO, table, left)
+        pl.when(edge[0] != 1)(lambda: build_rows(p_prev, 0, table, left))
+        pl.when(edge[0] != 2)(lambda: build_rows(p_next, HALO, table, left))
         table[0] = jnp.zeros((BS, 128), jnp.bfloat16)
 
-    def rows(it, carry):
+    def rows(low, high, it, carry):
         kept = []
         for u in range(UNROLL + 1):
             if u < UNROLL:
@@ -143,8 +213,8 @@
                 i = step * GROUP + r
                 halves = []
                 for nt in range(2):
-                    weights = coefficients(table, codes, i, 2, nt, left)
-                    total = jnp.dot(a_ref[r], weights, preferred_element_type=jnp.float32)
+                    weights = coefficients(table, codes, low * KC * FB + i, high - low, nt, left)
+                    total = jnp.dot(a_ref[r, :, low * BS:high * BS], weights, preferred_element_type=jnp.float32)
                     total = total + part_ref[r, :, nt * 256:(nt + 1) * 256].astype(jnp.float32)
                     halves.append(total.astype(jnp.bfloat16))
                 kept.append(jnp.concatenate(halves, axis=1))
@@ -158,7 +228,10 @@
                     acc[to] += pieces[m * BS:(m + 1) * BS]
         return carry
 
-    lax.fori_loop(0, GROUP // UNROLL, rows, 0)
+    for kind, (low, high) in enumerate(((0, 2), (1, 2), (0, 1))):
+        @pl.when(edge[0] == kind)
+        def _(low=low, high=high):
+            lax.fori_loop(0, GROUP // UNROLL, functools.partial(rows, low, high), 0)
 
     @pl.when(step == MAIN_STEPS - 1)
     def _():
@@ -167,13 +240,13 @@
         next_ref[...] = acc[2 * CB:3 * CB].astype(jnp.bfloat16)
 
 
-def halo_part(codes, touch, targets, p_prev, p_next, part, a_blocks, p_local):
+def halo_part(codes, touch, targets, edge, p_prev, p_next, part, a_blocks, p_local):
     whole = lambda s, *_: (0, 0, 0)
     rows = (CB, BS, KC * BS)
     return pl.pallas_call(
         halo_kernel,
         grid_spec=pltpu.PrefetchScalarGridSpec(
-            num_scalar_prefetch=3,
+            num_scalar_prefetch=4,
             grid=(MAIN_STEPS,),
             in_specs=[
                 pl.BlockSpec((HALO, BS, KP * BS), whole),
@@ -195,7 +268,7 @@
         ],
         compiler_params=pltpu.CompilerParams(vmem_limit_bytes=49 * 1024 * 1024),
         cost_estimate=pl.CostEstimate(flops=16_000_000_000, bytes_accessed=20_000_000, transcendentals=0),
-    )(codes, touch, targets, p_prev, p_next, part, a_blocks, p_local)
+    )(codes, touch, targets, edge, p_prev, p_next, part, a_blocks, p_local)
 
 
 def exchange_kernel(n_grp, n_dev, own_hbm, prev_ref, next_ref, out_ref, own_ref, from_prev, from_next, sems_out,
@@ -303,11 +376,6 @@
     axes = ("grp", "dev")
     position = lax.axis_index(axes)
     count = lax.axis_size(axes)
-    up = [(i, i + 1) for i in range(count - 1)]
-    down = [(j, i) for i, j in up]
-    p_prev = lax.ppermute(p_blocks[FB - HALO:], axes, up)
-    p_next = lax.ppermute(p_blocks[:HALO], axes, down)
-
     local = a_cols.T - position * FB
     slots = ap_slots.T.reshape(KA, KP, FB)
     weights = jnp.int32(1) << jnp.arange(KP, dtype=jnp.int32)
@@ -318,10 +386,10 @@
     nearby = jnp.where(local < 0, local + HALO, local - FB + HALO)[KA - 2:, None, :]
     subset, inside = subset[KA - 2:], inside[KA - 2:, None, :]
     there = jnp.where((subset == 0) | inside, 0, nearby * SUBSETS + subset)
-    edge = ((position == 0) | (position == count - 1)).astype(jnp.int32).reshape(1)
+    edge = jnp.where(position == 0, 1, jnp.where(position == count - 1, 2, 0)).astype(jnp.int32).reshape(1)
     targets = (owner_dev[:, 0] - position + 1) * CB + owner_row
-    part = local_part(here.reshape(-1), edge, p_blocks, a_blocks)
-    own, to_prev, to_next = halo_part(there.reshape(-1), p_touch.T.reshape(-1), targets, p_prev, p_next, part,
+    part, p_prev, p_next = local_part(here.reshape(-1), p_blocks, a_blocks)
+    own, to_prev, to_next = halo_part(there.reshape(-1), p_touch.T.reshape(-1), targets, edge, p_prev, p_next, part,
                                       a_blocks, p_blocks)
     return exchange(own, to_prev, to_next)
 

time: 100 us -> 96.6 us (0.966)
  starting transfers between devices: 4.38 us -> 0 us
  other arithmetic: 0.74 us -> 4.2 us
  Pallas kernels: 90.8 us -> 88.1 us
    ppermute x2 -> x0, starting transfers between devices: 4.38 us -> none  [the longest x1 3.1 us: on_device(): p_prev = lax.ppermute(p_blocks[FB - HALO:], axes, up)]
    slice x1 -> x0, local copies, waits for them, and re-layouts: 2.76 us -> none  [on_device(): p_next = lax.ppermute(p_blocks[:HALO], axes, down)]
    unnamed x11 -> x7, local copies, waits for them, and re-layouts: 1.34 us -> 3.77 us
    pallas_call x1, Pallas kernels: 31.6 us -> 30.3 us  [local_part(): pl.pallas_call(functools.partial(local_kernel, n_grp, n_dev), grid_spec=p...]
    pallas_call x1, Pallas kernels: 24.7 us -> 23.7 us  [halo_part(): pl.pallas_call(halo_kernel, grid_spec=pltpu.PrefetchScalarGridSpec(num_sc...]
  transfers between devices with their start and end apart: 2 -> 0, of which waited for: 0 -> 0; matrix products, arithmetic and copies ran while one was open for 1% -> 0% of each run, Pallas kernels for 32% -> 0%
where the time goes in v4:
time: 96.6 us; the launch traced here: 96.2 us
  Pallas kernels  88.1 us (91%)
  other arithmetic  4.2 us (4%)
  local copies, waits for them, and re-layouts  3.78 us (4%)
    pallas_call x1, Pallas kernels, exchange(): pl.pallas_call(functools.partial(exchange_kernel, n_grp, n_dev), out_shap...  34.2 us
    pallas_call x1, Pallas kernels, local_part(): pl.pallas_call(functools.partial(local_kernel, n_grp, n_dev), grid_spec=p...  30.3 us
    pallas_call x1, Pallas kernels, halo_part(): pl.pallas_call(halo_kernel, grid_spec=pltpu.PrefetchScalarGridSpec(num_sc...  23.7 us
    unnamed x7, local copies, waits for them, and re-layouts  3.77 us

profile of v4, /device:TPU:0, one launch (start us, length us, event | category | flops | bytes accessed | tf_op | source)
XLA Modules:
  0.0 96.2 jit_solution(6220585186985834155)
XLA Ops:
  0.0 0.7 add_multiply_fusion
  0.7 0.7 add.52.targets
  1.4 0.7 fusion
  2.1 0.7 multiply_bitcast_fusion
  2.8 0.8 select_reduce_fusion
  3.6 0.6 select_bitcast_fusion.codes
  4.2 0.0 copy-start
  4.2 30.3 %shard_map.73 = (bf16[128,64,512]{2,1,0:T(8,128)(2,1)}, bf16[32,64,256]{2,1,0:T(8,128)(2,1)}, bf16[32,64,256]{2,1,0:T(8,128)(2,1)}) custom-call(s32[8192]{0:T(1024)} %select_bitcast_fusion.codes, bf16[128,64,256]{2,1,0:T(8,128)(2,1)} %p_ref.3, bf16[128,64,256]{2,1,0:T(8,128)(2,1)} %p_ref.3, bf16[128,64,512]{2,1,0:T(8,128)(2,1)} %a_ref.3), custom_call_target="tpu_custom_call" | custom-call | flops 16000000000 | bytes 20000000 | tf_op jit(solution)/shard_map/pallas_call | solution.py:169
  34.6 0.0 copy-done
  34.6 0.0 copy-start.1
  34.6 1.2 %copy-done.1 = bf16[32,64,256]{2,1,0:T(8,128)(2,1)S(1)} copy-done((bf16[32,64,256]{2,1,0:T(8,128)(2,1)S(1)}, bf16[32,64,256]{2,1,0:T(8,128)(2,1)}, u32[]{:S(2)}) %copy-start.1) | copy-done | bytes 1048600
  35.8 0.0 copy-start.2
  35.8 1.2 %copy-done.2 = bf16[32,64,256]{2,1,0:T(8,128)(2,1)S(1)} copy-done((bf16[32,64,256]{2,1,0:T(8,128)(2,1)S(1)}, bf16[32,64,256]{2,1,0:T(8,128)(2,1)}, u32[]{:S(2)}) %copy-start.2) | copy-done | bytes 1048600
  37.0 23.7 %shard_map.74 = (f32[8,64,512]{2,1,0:T(8,128)S(1)}, bf16[8,64,512]{2,1,0:T(8,128)(2,1)S(1)}, bf16[8,64,512]{2,1,0:T(8,128)(2,1)S(1)}) custom-call(s32[2048]{0:T(1024)S(1)} %select_bitcast_fusion.1.codes, s32[512]{0:T(512)S(1)} %bitcast.19, s32[224]{0:T(256)S(1)} %add.52.targets, s32[1]{0:T(128)} %bitcast.8.edge, bf16[32,64,256]{2,1,0:T(8,128)(2,1)S(1)} %copy-done.1, ...), custom_call_target="tpu_custom_call" | custom-call | flops 16000000000 | bytes 20000000 | tf_op jit(solution)/shard_map/pallas_call | solution.py:246
  60.7 34.2 %shard_map.75 = bf16[32,64,512]{2,1,0:T(8,128)(2,1)S(1)} custom-call(f32[8,64,512]{2,1,0:T(8,128)S(1)} %get-tuple-element.14.own_hbm, bf16[8,64,512]{2,1,0:T(8,128)(2,1)S(1)} %get-tuple-element.15.prev_ref, bf16[8,64,512]{2,1,0:T(8,128)(2,1)S(1)} %get-tuple-element.16.next_ref), custom_call_target="tpu_custom_call" | custom-call | tf_op jit(solution)/shard_map/pallas_call | solution.py:357
  94.9 1.3 %copy.9 = bf16[32,64,512]{2,1,0:T(8,128)(2,1)} copy(bf16[32,64,512]{2,1,0:T(8,128)(2,1)S(1)} %shard_map.75) | data formatting | bytes 4194304
  (4 shorter events, 0.0 us)
Async XLA Ops:
  4.2 30.3 %copy-start = (s32[128,4]{0,1:T(4,128)S(1)}, s32[128,4]{0,1:T(4,128)}, u32[]{:S(2)}) copy-start(s32[128,4]{0,1:T(4,128)} %param.11) | copy-start | bytes 6148
  34.6 1.2 %copy-start.1 = (bf16[32,64,256]{2,1,0:T(8,128)(2,1)S(1)}, bf16[32,64,256]{2,1,0:T(8,128)(2,1)}, u32[]{:S(2)}) copy-start(bf16[32,64,256]{2,1,0:T(8,128)(2,1)} %get-tuple-element.11.p_prev) | copy-start | bytes 3145732
  35.8 1.2 %copy-start.2 = (bf16[32,64,256]{2,1,0:T(8,128)(2,1)S(1)}, bf16[32,64,256]{2,1,0:T(8,128)(2,1)}, u32[]{:S(2)}) copy-start(bf16[32,64,256]{2,1,0:T(8,128)(2,1)} %get-tuple-element.12.p_next) | copy-start | bytes 3145732

commit v5 on v4

--- a/solution.py
+++ b/solution.py
@@ -20,6 +20,7 @@
 LOCAL_STEPS = FB // P_ROWS
 GROUP = 16
 UNROLL = 8
+LOCAL_UNROLL = 16
 SEND_STEP = 2
 MAIN_STEPS = FB // GROUP
 TARGETS = 3 * CB
@@ -47,20 +48,48 @@
             table[at + subset] = value.astype(jnp.bfloat16)
         return carry
 
-    lax.fori_loop(0, P_ROWS, row, 0, unroll=4)
+    lax.fori_loop(0, P_ROWS, row, 0, unroll=8)
+
+
+def codes_kernel(place, cols_ref, slots_ref, codes_ref):
+    each = lax.broadcasted_iota(jnp.int32, (KC, FB), 0)
+    for k in range(KA):
+        local = cols_ref[k:k + 1, :] - place[0] * FB
+        subset = jnp.zeros((KC, FB), jnp.int32)
+        for m in range(KP):
+            at = k * KP + m
+            subset = subset + jnp.where(slots_ref[at:at + 1, :] == each, 1 << m, 0)
+        nearby = jnp.where(local < 0, local + HALO, local - FB + HALO)
+        here = (local >= 0) & (local < FB)
+        row = jnp.where(here, local, nearby) * SUBSETS + subset
+        code = jnp.where(here, row, -row)
+        codes_ref[k * KC:(k + 1) * KC, :] = jnp.where(subset == 0, 0, code)
+
+
+def table_codes(place, cols, slots):
+    return pl.pallas_call(
+        codes_kernel,
+        in_specs=[
+            pl.BlockSpec(memory_space=pltpu.SMEM),
+            pl.BlockSpec(memory_space=pltpu.VMEM),
+            pl.BlockSpec(memory_space=pltpu.VMEM),
+        ],
+        out_specs=pl.BlockSpec(memory_space=pltpu.VMEM),
+        out_shape=jax.ShapeDtypeStruct((KA * KC, FB), jnp.int32),
+        compiler_params=pltpu.CompilerParams(vmem_limit_bytes=63 * 1024 * 1024),
+    )(place, cols, slots)
 
 
 def left_half():
     return lax.broadcasted_iota(jnp.int32, (BS, 128), 1) < 64
 
 
-def coefficients(table, codes, first, blocks, nt, left):
+def coefficients(table, index, low, high, nt, left):
     rows = []
-    for k in range(blocks):
+    for k in range(low, high):
         tiles = []
         for s in range(4 * nt, 4 * nt + 4, 2):
-            at = (k * KC + s) * FB + first
-            tiles.append(jnp.where(left, table[codes[at]], table[codes[at + FB]]))
+            tiles.append(jnp.where(left, table[index(k, s)], table[index(k, s + 1)]))
         rows.append(jnp.concatenate(tiles, axis=1))
     return jnp.concatenate(rows, axis=0)
 
@@ -123,19 +152,24 @@
         first = (step - LOCAL_STEPS) * GROUP
 
         def rows(it, carry):
-            for u in range(UNROLL):
-                r = it * UNROLL + u
+            for u in range(LOCAL_UNROLL):
+                r = it * LOCAL_UNROLL + u
+
+                def index(k, s, i=first + r):
+                    code = codes[(k * KC + s) * FB + i]
+                    return code if k < KA - 2 else jnp.maximum(code, 0)
+
                 for nt in range(2):
                     total = None
                     for low, high in cuts:
-                        weights = coefficients(table, codes, low * KC * FB + first + r, high - low, nt, left)
+                        weights = coefficients(table, index, low, high, nt, left)
                         part = jnp.dot(a_ref[r, :, low * BS:high * BS], weights,
                                        preferred_element_type=jnp.float32)
                         total = part if total is None else total + part
                     out_ref[r, :, nt * 256:(nt + 1) * 256] = total.astype(jnp.bfloat16)
             return carry
 
-        lax.fori_loop(0, GROUP // UNROLL, rows, 0)
+        lax.fori_loop(0, GROUP // LOCAL_UNROLL, rows, 0)
 
     @pl.when((step >= LOCAL_STEPS) & has_before & has_after)
     def _():
@@ -193,16 +227,18 @@
     )(codes, p_local, p_local, a_blocks)
 
 
-def halo_kernel(codes, touch, targets, edge, p_prev, p_next, part_ref, a_ref, p_ref, own_ref, prev_ref, next_ref,
+def halo_kernel(count, codes, touch, owner_dev, owner_row, place, p_prev, p_next, part_ref, a_ref, p_ref, own_ref, prev_ref, next_ref,
                 table, acc):
     step = pl.program_id(0)
     left = left_half()
+    position = place[0]
+    is_first, is_last = position == 0, position == count - 1
 
     @pl.when(step == 0)
     def _():
         acc[...] = jnp.zeros_like(acc)
-        pl.when(edge[0] != 1)(lambda: build_rows(p_prev, 0, table, left))
-        pl.when(edge[0] != 2)(lambda: build_rows(p_next, HALO, table, left))
+        pl.when(~is_first)(lambda: build_rows(p_prev, 0, table, left))
+        pl.when(~is_last)(lambda: build_rows(p_next, HALO, table, left))
         table[0] = jnp.zeros((BS, 128), jnp.bfloat16)
 
     def rows(low, high, it, carry):
@@ -212,8 +248,12 @@
                 r = it * UNROLL + u
                 i = step * GROUP + r
                 halves = []
+
+                def index(k, s, i=i):
+                    return jnp.maximum(-codes[((KA - 2 + k) * KC + s) * FB + i], 0)
+
                 for nt in range(2):
-                    weights = coefficients(table, codes, low * KC * FB + i, high - low, nt, left)
+                    weights = coefficients(table, index, low, high, nt, left)
                     total = jnp.dot(a_ref[r, :, low * BS:high * BS], weights, preferred_element_type=jnp.float32)
                     total = total + part_ref[r, :, nt * 256:(nt + 1) * 256].astype(jnp.float32)
                     halves.append(total.astype(jnp.bfloat16))
@@ -224,12 +264,13 @@
                 pieces = lax.dot_general(p_ref[r], kept[u - 1], (((0,), (0,)), ((), ())),
                                          preferred_element_type=jnp.float32)
                 for m in range(KP):
-                    to = targets[touch[m * FB + i]]
+                    t = touch[m * FB + i]
+                    to = (owner_dev[t] - position + 1) * CB + owner_row[t]
                     acc[to] += pieces[m * BS:(m + 1) * BS]
         return carry
 
-    for kind, (low, high) in enumerate(((0, 2), (1, 2), (0, 1))):
-        @pl.when(edge[0] == kind)
+    for when, low, high in ((~is_first & ~is_last, 0, 2), (is_first, 1, 2), (is_last, 0, 1)):
+        @pl.when(when)
         def _(low=low, high=high):
             lax.fori_loop(0, GROUP // UNROLL, functools.partial(rows, low, high), 0)
 
@@ -240,13 +281,13 @@
         next_ref[...] = acc[2 * CB:3 * CB].astype(jnp.bfloat16)
 
 
-def halo_part(codes, touch, targets, edge, p_prev, p_next, part, a_blocks, p_local):
+def halo_part(codes, touch, owner_dev, owner_row, place, p_prev, p_next, part, a_blocks, p_local):
     whole = lambda s, *_: (0, 0, 0)
     rows = (CB, BS, KC * BS)
     return pl.pallas_call(
-        halo_kernel,
+        functools.partial(halo_kernel, lax.axis_size("grp") * lax.axis_size("dev")),
         grid_spec=pltpu.PrefetchScalarGridSpec(
-            num_scalar_prefetch=4,
+            num_scalar_prefetch=5,
             grid=(MAIN_STEPS,),
             in_specs=[
                 pl.BlockSpec((HALO, BS, KP * BS), whole),
@@ -266,9 +307,9 @@
             jax.ShapeDtypeStruct(rows, jnp.bfloat16),
             jax.ShapeDtypeStruct(rows, jnp.bfloat16),
         ],
-        compiler_params=pltpu.CompilerParams(vmem_limit_bytes=49 * 1024 * 1024),
+        compiler_params=pltpu.CompilerParams(vmem_limit_bytes=51 * 1024 * 1024),
         cost_estimate=pl.CostEstimate(flops=16_000_000_000, bytes_accessed=20_000_000, transcendentals=0),
-    )(codes, touch, targets, edge, p_prev, p_next, part, a_blocks, p_local)
+    )(codes, touch, owner_dev, owner_row, place, p_prev, p_next, part, a_blocks, p_local)
 
 
 def exchange_kernel(n_grp, n_dev, own_hbm, prev_ref, next_ref, out_ref, own_ref, from_prev, from_next, sems_out,
@@ -375,22 +416,11 @@
 def on_device(a_blocks, a_cols, p_blocks, ap_slots, p_touch, owner_dev, owner_row):
     axes = ("grp", "dev")
     position = lax.axis_index(axes)
-    count = lax.axis_size(axes)
-    local = a_cols.T - position * FB
-    slots = ap_slots.T.reshape(KA, KP, FB)
-    weights = jnp.int32(1) << jnp.arange(KP, dtype=jnp.int32)
-    hits = slots[:, :, None, :] == jnp.arange(KC, dtype=jnp.int32)[:, None]
-    subset = jnp.sum(jnp.where(hits, weights[:, None, None], 0), axis=1)
-    inside = (local >= 0) & (local < FB)
-    here = jnp.where((subset == 0) | ~inside[:, None, :], 0, local[:, None, :] * SUBSETS + subset)
-    nearby = jnp.where(local < 0, local + HALO, local - FB + HALO)[KA - 2:, None, :]
-    subset, inside = subset[KA - 2:], inside[KA - 2:, None, :]
-    there = jnp.where((subset == 0) | inside, 0, nearby * SUBSETS + subset)
-    edge = jnp.where(position == 0, 1, jnp.where(position == count - 1, 2, 0)).astype(jnp.int32).reshape(1)
-    targets = (owner_dev[:, 0] - position + 1) * CB + owner_row
-    part, p_prev, p_next = local_part(here.reshape(-1), p_blocks, a_blocks)
-    own, to_prev, to_next = halo_part(there.reshape(-1), p_touch.T.reshape(-1), targets, edge, p_prev, p_next, part,
-                                      a_blocks, p_blocks)
+    place = position.astype(jnp.int32).reshape(1)
+    codes = table_codes(place, a_cols.T, ap_slots.T).reshape(-1)
+    part, p_prev, p_next = local_part(codes, p_blocks, a_blocks)
+    own, to_prev, to_next = halo_part(codes, p_touch.T.reshape(-1), owner_dev.reshape(-1), owner_row,
+                                      place, p_prev, p_next, part, a_blocks, p_blocks)
     return exchange(own, to_prev, to_next)
 
 

time: 96.6 us -> 89.8 us (0.930)
  other arithmetic: 4.2 us -> 0 us
  local copies, waits for them, and re-layouts: 3.78 us -> 1.34 us
    unnamed x7 -> x9, local copies, waits for them, and re-layouts: 3.77 us -> 1.34 us
    pallas_call x1 -> x2, Pallas kernels: 23.7 us -> 25.8 us  [the longest x1 24.4 us: halo_part(): pl.pallas_call(functools.partial(halo_kernel, lax.axis_size('grp') * lax....]
    pallas_call x1, Pallas kernels: 30.3 us -> 28.2 us  [local_part(): pl.pallas_call(functools.partial(local_kernel, n_grp, n_dev), grid_spec=p...]
    mul x3 -> x0, other arithmetic: 1.38 us -> none  [the longest x1 0.69 us: on_device(): local[:, None, :] * SUBSETS + subset]
where the time goes in v5:
time: 89.8 us; the launch traced here: 89.6 us
  Pallas kernels  88.2 us (98%)
  local copies, waits for them, and re-layouts  1.34 us (1%)
    pallas_call x1, Pallas kernels, exchange(): pl.pallas_call(functools.partial(exchange_kernel, n_grp, n_dev), out_shap...  34.2 us
    pallas_call x1, Pallas kernels, local_part(): pl.pallas_call(functools.partial(local_kernel, n_grp, n_dev), grid_spec=p...  28.2 us
    pallas_call x1, Pallas kernels, halo_part(): pl.pallas_call(functools.partial(halo_kernel, lax.axis_size('grp') * lax....  24.4 us

profile of v5, /device:TPU:0, one launch (start us, length us, event | category | flops | bytes accessed | tf_op | source)
XLA Modules:
  0.0 89.6 jit_solution(6703989809026905195)
XLA Ops:
  0.0 1.4 %shard_map.73 = s32[64,128]{1,0:T(8,128)} custom-call(s32[1]{0:T(128)} %bitcast.place, s32[8,128]{1,0:T(8,128)} %bitcast.13, s32[32,128]{1,0:T(8,128)} %bitcast.12), custom_call_target="tpu_custom_call" | custom-call | tf_op jit(solution)/shard_map/pallas_call | solution.py:70
  1.4 0.0 copy-start
  1.4 0.0 copy-start.1
  1.4 0.0 copy-start.2
  1.4 0.0 copy-start.3
  1.4 28.2 %shard_map.74 = (bf16[128,64,512]{2,1,0:T(8,128)(2,1)}, bf16[32,64,256]{2,1,0:T(8,128)(2,1)}, bf16[32,64,256]{2,1,0:T(8,128)(2,1)}) custom-call(s32[8192]{0:T(1024)} %bitcast.8, bf16[128,64,256]{2,1,0:T(8,128)(2,1)} %p_ref.3, bf16[128,64,256]{2,1,0:T(8,128)(2,1)} %p_ref.3, bf16[128,64,512]{2,1,0:T(8,128)(2,1)} %a_ref.3), custom_call_target="tpu_custom_call" | custom-call | flops 16000000000 | bytes 20000000 | tf_op jit(solution)/shard_map/pallas_call | solution.py:203
  29.6 0.0 copy-done
  29.6 0.0 copy-done.1
  29.6 0.0 copy-done.2
  29.6 0.0 copy-done.3
  29.6 24.4 %shard_map.75 = (f32[8,64,512]{2,1,0:T(8,128)S(1)}, bf16[8,64,512]{2,1,0:T(8,128)(2,1)S(1)}, bf16[8,64,512]{2,1,0:T(8,128)(2,1)S(1)}) custom-call(s32[8192]{0:T(1024)S(1)} %bitcast.9, s32[512]{0:T(512)S(1)} %bitcast.10, s32[224]{0:T(256)S(1)} %bitcast.11, s32[224]{0:T(256)S(1)} %copy-done.3, s32[1]{0:T(128)} %bitcast.place, ...), custom_call_target="tpu_custom_call" | custom-call | flops 16000000000 | bytes 20000000 | tf_op jit(solution)/shard_map/pallas_call | solution.py:287
  54.1 34.2 %shard_map.76 = bf16[32,64,512]{2,1,0:T(8,128)(2,1)S(1)} custom-call(f32[8,64,512]{2,1,0:T(8,128)S(1)} %get-tuple-element.14.own_hbm, bf16[8,64,512]{2,1,0:T(8,128)(2,1)S(1)} %get-tuple-element.15.prev_ref, bf16[8,64,512]{2,1,0:T(8,128)(2,1)S(1)} %get-tuple-element.16.next_ref), custom_call_target="tpu_custom_call" | custom-call | tf_op jit(solution)/shard_map/pallas_call | solution.py:398
  88.2 1.3 %copy.9 = bf16[32,64,512]{2,1,0:T(8,128)(2,1)} copy(bf16[32,64,512]{2,1,0:T(8,128)(2,1)S(1)} %shard_map.76) | data formatting | bytes 4194304
Async XLA Ops:
  1.4 28.2 %copy-start = (s32[64,128]{1,0:T(8,128)S(1)}, s32[64,128]{1,0:T(8,128)}, u32[]{:S(2)}) copy-start(s32[64,128]{1,0:T(8,128)} %shard_map.73) | copy-start | bytes 98308
  1.4 28.2 %copy-start.1 = (s32[128,4]{0,1:T(4,128)S(1)}, s32[128,4]{0,1:T(4,128)}, u32[]{:S(2)}) copy-start(s32[128,4]{0,1:T(4,128)} %param.11) | copy-start | bytes 6148
  1.4 28.2 %copy-start.2 = (s32[224,1]{0,1:T(1,128)S(1)}, s32[224,1]{0,1:T(1,128)}, u32[]{:S(2)}) copy-start(s32[224,1]{0,1:T(1,128)} %param.12) | copy-start | bytes 2692
  1.4 28.2 %copy-start.3 = (s32[224]{0:T(256)S(1)}, s32[224]{0:T(256)}, u32[]{:S(2)}) copy-start(s32[224]{0:T(256)} %owner_row.1) | copy-start | bytes 2692

commit v6 on v5

--- a/solution.py
+++ b/solution.py
@@ -19,8 +19,9 @@
 P_ROWS = 32
 LOCAL_STEPS = FB // P_ROWS
 GROUP = 16
-UNROLL = 8
 LOCAL_UNROLL = 16
+HALO_UNROLL = 16
+LAG = 2
 SEND_STEP = 2
 MAIN_STEPS = FB // GROUP
 TARGETS = 3 * CB
@@ -48,7 +49,7 @@
             table[at + subset] = value.astype(jnp.bfloat16)
         return carry
 
-    lax.fori_loop(0, P_ROWS, row, 0, unroll=8)
+    lax.fori_loop(0, P_ROWS, row, 0, unroll=16)
 
 
 def codes_kernel(place, cols_ref, slots_ref, codes_ref):
@@ -181,7 +182,7 @@
 
     @pl.when((step >= LOCAL_STEPS) & ~has_after)
     def _():
-        assemble(((0, 4), (4, KA)))
+        assemble(((0, 4), (4, KA - 2), (KA - 1, KA)))
 
     last = LOCAL_STEPS + MAIN_STEPS - 1
 
@@ -243,9 +244,9 @@
 
     def rows(low, high, it, carry):
         kept = []
-        for u in range(UNROLL + 1):
-            if u < UNROLL:
-                r = it * UNROLL + u
+        for u in range(HALO_UNROLL + LAG):
+            if u < HALO_UNROLL:
+                r = it * HALO_UNROLL + u
                 i = step * GROUP + r
                 halves = []
 
@@ -258,10 +259,10 @@
                     total = total + part_ref[r, :, nt * 256:(nt + 1) * 256].astype(jnp.float32)
                     halves.append(total.astype(jnp.bfloat16))
                 kept.append(jnp.concatenate(halves, axis=1))
-            if u >= 1:
-                r = it * UNROLL + u - 1
+            if u >= LAG:
+                r = it * HALO_UNROLL + u - LAG
                 i = step * GROUP + r
-                pieces = lax.dot_general(p_ref[r], kept[u - 1], (((0,), (0,)), ((), ())),
+                pieces = lax.dot_general(p_ref[r], kept[u - LAG], (((0,), (0,)), ((), ())),
                                          preferred_element_type=jnp.float32)
                 for m in range(KP):
                     t = touch[m * FB + i]
@@ -272,7 +273,7 @@
     for when, low, high in ((~is_first & ~is_last, 0, 2), (is_first, 1, 2), (is_last, 0, 1)):
         @pl.when(when)
         def _(low=low, high=high):
-            lax.fori_loop(0, GROUP // UNROLL, functools.partial(rows, low, high), 0)
+            lax.fori_loop(0, GROUP // HALO_UNROLL, functools.partial(rows, low, high), 0)
 
     @pl.when(step == MAIN_STEPS - 1)
     def _():

time: 89.8 us -> 83.2 us (0.927)
  Pallas kernels: 88.2 us -> 81.5 us
    pallas_call x1, Pallas kernels: 24.4 us -> 18.7 us  [halo_part(): pl.pallas_call(functools.partial(halo_kernel, lax.axis_size('grp') * lax....]
where the time goes in v6:
time: 83.2 us; the launch traced here: 82.9 us
  Pallas kernels  81.5 us (98%)
  local copies, waits for them, and re-layouts  1.34 us (2%)
    pallas_call x1, Pallas kernels, exchange(): pl.pallas_call(functools.partial(exchange_kernel, n_grp, n_dev), out_shap...  33.7 us
    pallas_call x1, Pallas kernels, local_part(): pl.pallas_call(functools.partial(local_kernel, n_grp, n_dev), grid_spec=p...  27.7 us
    pallas_call x1, Pallas kernels, halo_part(): pl.pallas_call(functools.partial(halo_kernel, lax.axis_size('grp') * lax....  18.7 us

profile of v6, /device:TPU:0, one launch (start us, length us, event | category | flops | bytes accessed | tf_op | source)
XLA Modules:
  0.0 82.9 jit_solution(2711565492997971024)
XLA Ops:
  0.0 1.4 %shard_map.73 = s32[64,128]{1,0:T(8,128)} custom-call(s32[1]{0:T(128)} %bitcast.place, s32[8,128]{1,0:T(8,128)} %bitcast.13, s32[32,128]{1,0:T(8,128)} %bitcast.12), custom_call_target="tpu_custom_call" | custom-call | tf_op jit(solution)/shard_map/pallas_call | solution.py:71
  1.4 0.0 copy-start
  1.4 0.0 copy-start.1
  1.4 0.0 copy-start.2
  1.4 0.0 copy-start.3
  1.4 27.7 %shard_map.74 = (bf16[128,64,512]{2,1,0:T(8,128)(2,1)}, bf16[32,64,256]{2,1,0:T(8,128)(2,1)}, bf16[32,64,256]{2,1,0:T(8,128)(2,1)}) custom-call(s32[8192]{0:T(1024)} %bitcast.8, bf16[128,64,256]{2,1,0:T(8,128)(2,1)} %p_ref.3, bf16[128,64,256]{2,1,0:T(8,128)(2,1)} %p_ref.3, bf16[128,64,512]{2,1,0:T(8,128)(2,1)} %a_ref.3), custom_call_target="tpu_custom_call" | custom-call | flops 16000000000 | bytes 20000000 | tf_op jit(solution)/shard_map/pallas_call | solution.py:204
  29.1 0.0 copy-done
  29.1 0.0 copy-done.1
  29.1 0.0 copy-done.2
  29.1 0.0 copy-done.3
  29.1 18.7 %shard_map.75 = (f32[8,64,512]{2,1,0:T(8,128)S(1)}, bf16[8,64,512]{2,1,0:T(8,128)(2,1)S(1)}, bf16[8,64,512]{2,1,0:T(8,128)(2,1)S(1)}) custom-call(s32[8192]{0:T(1024)S(1)} %bitcast.9, s32[512]{0:T(512)S(1)} %bitcast.10, s32[224]{0:T(256)S(1)} %bitcast.11, s32[224]{0:T(256)S(1)} %copy-done.3, s32[1]{0:T(128)} %bitcast.place, ...), custom_call_target="tpu_custom_call" | custom-call | flops 16000000000 | bytes 20000000 | tf_op jit(solution)/shard_map/pallas_call | solution.py:288
  47.8 33.7 %shard_map.76 = bf16[32,64,512]{2,1,0:T(8,128)(2,1)S(1)} custom-call(f32[8,64,512]{2,1,0:T(8,128)S(1)} %get-tuple-element.14.own_hbm, bf16[8,64,512]{2,1,0:T(8,128)(2,1)S(1)} %get-tuple-element.15.prev_ref, bf16[8,64,512]{2,1,0:T(8,128)(2,1)S(1)} %get-tuple-element.16.next_ref), custom_call_target="tpu_custom_call" | custom-call | tf_op jit(solution)/shard_map/pallas_call | solution.py:399
  81.5 1.3 %copy.9 = bf16[32,64,512]{2,1,0:T(8,128)(2,1)} copy(bf16[32,64,512]{2,1,0:T(8,128)(2,1)S(1)} %shard_map.76) | data formatting | bytes 4194304
Async XLA Ops:
  1.4 27.7 %copy-start = (s32[64,128]{1,0:T(8,128)S(1)}, s32[64,128]{1,0:T(8,128)}, u32[]{:S(2)}) copy-start(s32[64,128]{1,0:T(8,128)} %shard_map.73) | copy-start | bytes 98308
  1.4 27.7 %copy-start.1 = (s32[128,4]{0,1:T(4,128)S(1)}, s32[128,4]{0,1:T(4,128)}, u32[]{:S(2)}) copy-start(s32[128,4]{0,1:T(4,128)} %param.11) | copy-start | bytes 6148
  1.4 27.7 %copy-start.2 = (s32[224,1]{0,1:T(1,128)S(1)}, s32[224,1]{0,1:T(1,128)}, u32[]{:S(2)}) copy-start(s32[224,1]{0,1:T(1,128)} %param.12) | copy-start | bytes 2692
  1.4 27.7 %copy-start.3 = (s32[224]{0:T(256)S(1)}, s32[224]{0:T(256)}, u32[]{:S(2)}) copy-start(s32[224]{0:T(256)} %owner_row.1) | copy-start | bytes 2692
